TPU v7x, 32 devices: a whole 2x2x4 slice. The times are simulated.
32 devices in a mesh: tm: 4 (over y, x), sx: 2 (over core), sy: 4 (over z).
Axes of the slice: x: 2, y: 2, z: 4, core: 2. Of those that a mesh axis runs over, the one named last changes fastest.
Arguments:
- driving_input: float32 [128, 8, 16, 512], P('tm', None, 'sx', 'sy'), may hold values from -4 to 4
- regime: int32 [8, 16, 512], P(None, 'sx', 'sy'), may hold values from 0 to 7
- reaction_rates: float32 [8], replicated, may hold values from 0.005 to 1
Outputs:
- solution: float32 [128, 8, 16, 512], P('tm', None, 'sx', 'sy')
All inputs are finite; a program needn't handle non-finite values.
Results may differ from a plain program's by a relative error of at most 0.00007.
Values sent between devices are 32-bit elements; how exact they have to be, the bound alone decides.
A program may use at most 64 MiB of HBM per device.

v0:
```python
import jax
import jax.numpy as jnp
from jax import lax
from jax.sharding import PartitionSpec as P

AGGREGATE_XCELLS = 8
AGGREGATE_YCELLS = 32
SWEEPS = 4


TWO_PI = 2.0 * 3.141592653589793


def extended(block, sides, width):
    for axis, dim in sides:
        count = lax.axis_size(axis)
        forward = [(i, i + 1) for i in range(count - 1)]
        backward = [(target, source) for source, target in forward]
        low = lax.ppermute(
            lax.slice_in_dim(block, block.shape[dim] - width, None, axis=dim), axis, forward
        )
        high = lax.ppermute(lax.slice_in_dim(block, 0, width, axis=dim), axis, backward)
        block = jnp.concatenate([low, block, high], axis=dim)
    return block


def angle_table(row_index, col_index, cycle_duration):
    product = row_index[:, None] * col_index[None, :] % cycle_duration
    angles = product.astype(jnp.float32) * (TWO_PI / cycle_duration)
    return (jnp.cos(angles), jnp.sin(angles))


def matmul(left_side, right_side):
    return jnp.dot(
        left_side, right_side, precision=lax.Precision.HIGHEST, preferred_element_type=jnp.float32
    )


def complex_mul(left_real, left_imag, pair):
    return jnp.stack(
        [left_real * pair[0] - left_imag * pair[1], left_real * pair[1] + left_imag * pair[0]]
    )


def neighbors(present_guess):
    padded = extended(present_guess, (("sx", 3), ("sy", 4)), 1)
    running = padded[:, :, :, 2:, 1:-1] + padded[:, :, :, :-2, 1:-1]
    running = running + padded[:, :, :, 1:-1, 2:] + padded[:, :, :, 1:-1, :-2]
    running = running + jnp.roll(present_guess, 1, axis=2) + jnp.roll(present_guess, -1, axis=2)
    return running


def local(driving_input, regime, reaction_rates):
    moment_count, third_axis_count, first_axis_count, second_axis_count = driving_input.shape
    temporal_spacing = lax.axis_size("tm")
    sy_size = lax.axis_size("sy")
    cycle_duration = moment_count * temporal_spacing
    unknowns_in_tile = third_axis_count * first_axis_count * second_axis_count
    processor_lines = driving_input.reshape(moment_count, unknowns_in_tile)
    owned_slice_number = lax.axis_index("tm") * moment_count + jnp.arange(
        moment_count, dtype=jnp.int32
    )
    all_index = jnp.arange(cycle_duration, dtype=jnp.int32)
    cos_rows, sin_rows = angle_table(owned_slice_number, all_index, cycle_duration)

    def forward(running, segment, offset):
        return jnp.stack([matmul(cos_rows, segment), -matmul(sin_rows, segment)])

    eigen_spectra = forward(
        jnp.zeros((2, moment_count, unknowns_in_tile), jnp.float32),
        lax.all_gather(processor_lines, "tm", axis=0, tiled=True),
        jnp.int32(0),
    )
    source_term = eigen_spectra.reshape(
        2, moment_count, third_axis_count, first_axis_count, second_axis_count
    )
    phase_angle = owned_slice_number.astype(jnp.float32) * (TWO_PI / cycle_duration)
    shift_real = (1.0 - jnp.cos(phase_angle))[:, None, None, None]
    shift_imag = jnp.sin(phase_angle)[:, None, None, None]
    reaction = jnp.zeros(regime.shape, jnp.float32)
    for regime_no in range(reaction_rates.shape[0]):
        reaction = reaction + jnp.where(
            regime == regime_no, reaction_rates[regime_no], jnp.zeros((), jnp.float32)
        )
    diag_real = reaction[None] + 6.0 + shift_real
    diag_imag = jnp.zeros_like(diag_real) + shift_imag
    modulus = diag_real * diag_real + diag_imag * diag_imag
    inverse_real = diag_real / modulus
    inverse_imag = -diag_imag / modulus
    present_guess = complex_mul(inverse_real, inverse_imag, source_term)
    for sweep_no in range(SWEEPS - 1):
        present_guess = complex_mul(
            inverse_real, inverse_imag, source_term + neighbors(present_guess)
        )
    applied = complex_mul(diag_real, diag_imag, present_guess) - neighbors(present_guess)
    residual = source_term - applied
    first_axis_teams = first_axis_count // AGGREGATE_XCELLS
    second_axis_teams = second_axis_count // AGGREGATE_YCELLS
    per_device = first_axis_teams * second_axis_teams

    def aggregate(values):
        leading = values.shape[:-3]
        blocks = values.reshape(
            leading
            + (
                third_axis_count,
                first_axis_teams,
                AGGREGATE_XCELLS,
                second_axis_teams,
                AGGREGATE_YCELLS,
            )
        )
        return jnp.sum(blocks, axis=(-5, -3, -1)).reshape(leading + (per_device,))

    coarse_right = jnp.transpose(aggregate(residual), (1, 0, 2))
    rate_sums = aggregate(reaction)
    shift_column = 1.0 - jnp.cos(phase_angle)
    face_count = 2 * (AGGREGATE_YCELLS * third_axis_count + AGGREGATE_XCELLS * third_axis_count)
    volume = AGGREGATE_XCELLS * AGGREGATE_YCELLS * third_axis_count
    spatial = lax.axis_size("sx") * sy_size
    slot_count = -(-moment_count // spatial)
    padding_rows = slot_count * spatial - moment_count
    padded_right = jnp.pad(coarse_right, ((0, padding_rows), (0, 0), (0, 0)))
    sum_copies = jnp.broadcast_to(rate_sums[None, None, :], (spatial, 1, per_device))
    shared_right, shared_sums = (
        lax.all_to_all(padded_right, ("sx", "sy"), split_axis=0, concat_axis=2, tiled=True),
        lax.all_to_all(sum_copies, ("sx", "sy"), split_axis=0, concat_axis=2, tiled=True),
    )
    spatial_rank = lax.axis_index("sx") * sy_size + lax.axis_index("sy")
    padded_shift = jnp.pad(shift_column, (0, padding_rows))
    slot_shift = lax.dynamic_slice_in_dim(padded_shift, spatial_rank * slot_count, slot_count, 0)
    sum_values = shared_sums[0, 0]
    coarse_total = sum_values.shape[0]
    position = jnp.arange(coarse_total, dtype=jnp.int32)
    device = position // per_device
    within = position % per_device
    coarse_x = device // sy_size * first_axis_teams + within // second_axis_teams
    coarse_y = device % sy_size * second_axis_teams + within % second_axis_teams
    x_gap = jnp.abs(coarse_x[:, None] - coarse_x[None, :])
    y_gap = jnp.abs(coarse_y[:, None] - coarse_y[None, :])
    coupling = -(AGGREGATE_YCELLS * third_axis_count) * ((x_gap == 1) & (y_gap == 0)).astype(
        jnp.float32
    )
    coupling = coupling - AGGREGATE_XCELLS * third_axis_count * (
        (x_gap == 0) & (y_gap == 1)
    ).astype(jnp.float32)
    identity = (position[:, None] == position[None, :]).astype(jnp.float32)
    diagonal = sum_values + face_count
    system = (
        coupling[None]
        + identity[None] * (diagonal[None, :] + volume * slot_shift[:, None])[:, None, :]
    )
    factor = jnp.linalg.cholesky(system)
    right_side = jnp.transpose(shared_right, (0, 2, 1))
    forward_sub = lax.linalg.triangular_solve(factor, right_side, left_side=True, lower=True)
    coarse = lax.linalg.triangular_solve(
        factor, forward_sub, left_side=True, lower=True, transpose_a=True
    )
    solved = jnp.transpose(coarse, (0, 2, 1))
    returned = lax.all_to_all(solved, ("sx", "sy"), split_axis=2, concat_axis=0, tiled=True)
    own_coarse = returned[:moment_count]
    local_part = jnp.transpose(own_coarse, (1, 0, 2)).reshape(
        2, moment_count, 1, first_axis_teams, 1, second_axis_teams, 1
    )
    spread_values = jnp.broadcast_to(
        local_part,
        (
            2,
            moment_count,
            third_axis_count,
            first_axis_teams,
            AGGREGATE_XCELLS,
            second_axis_teams,
            AGGREGATE_YCELLS,
        ),
    )
    present_guess = present_guess + spread_values.reshape(
        2, moment_count, third_axis_count, first_axis_count, second_axis_count
    )
    unrolled_array = present_guess.reshape(2, moment_count, unknowns_in_tile)

    def backward(running, segment, offset):
        return matmul(cos_rows, segment[0]) - matmul(sin_rows, segment[1])

    result = (
        backward(
            jnp.zeros((moment_count, unknowns_in_tile), jnp.float32),
            lax.all_gather(unrolled_array, "tm", axis=1, tiled=True),
            jnp.int32(0),
        )
        / cycle_duration
    )
    return result.reshape(driving_input.shape)


def solution(mesh):
    placed = (P("tm", None, "sx", "sy"), P(None, "sx", "sy"), P())
    return jax.shard_map(
        local, mesh=mesh, in_specs=placed, out_specs=P("tm", None, "sx", "sy"), check_vma=False
    )
```

profile of v0, /device:TPU:0, one launch (start us, length us, event | category | flops | bytes accessed | tf_op | source)
XLA Modules:
  0.0 442.5 jit_solution(4548532242196316922)
XLA Ops:
  16.0 6.3 %all-to-all-start = ((f32[8,1,4]{2,1,0:T(1,128)}), f32[8,1,4]{2,1,0:T(1,128)}, u32[]{:S(2)}, u32[]{:S(2)}) async-start(f32[8,1,4]{2,1,0:T(1,128)} %broadcast_in_dim.75), calls=%async_computation | async-start | bytes 8192 | tf_op jit(solution)/shard_map/all_to_all | solution.py:127
  24.3 40.7 %all-gather.3.cloned.1.call-done = f32[128,8192]{1,0:T(8,128)} async-done(((f32[32,8192]{1,0:T(8,128)}), f32[128,8192]{1,0:T(8,128)}) %all-gather.3.cloned.1.call-update) | async-done | bytes 4194320 | tf_op jit(solution)/shard_map/all_gather | solution.py:71
  100.4 5.3 %copy.97 = f32[2,32,8,10,1]{4,3,2,0,1:T(8,128)} copy(f32[2,32,8,10,1]{1,2,4,3,0:T(8,128)} %collective-permute-done.3) | data formatting | bytes 40960 | tf_op jit(solution)/shard_map/ppermute | solution.py:19
  105.7 5.2 %copy.95 = f32[2,32,8,10,1]{4,3,2,0,1:T(8,128)} copy(f32[2,32,8,10,1]{1,2,4,3,0:T(8,128)} %collective-permute-done.2) | data formatting | bytes 40960 | tf_op jit(solution)/shard_map/ppermute | solution.py:22
  110.9 8.1 %fusion.34 = f32[2,32,8,8,128]{4,3,2,0,1:T(8,128)S(1)} fusion(f32[1,32,8,8,128]{4,3,2,0,1:T(8,128)} %copy-done.3, f32[1,32,8,8,128]{4,3,2,0,1:T(8,128)S(1)} %get-tuple-element.22, f32[2,32,8,10,1]{4,3,2,0,1:T(8,128)} %copy.97, f32[2,32,8,1,128]{4,3,2,0,1:T(1,128)S(1)} %collective-permute-done, f32[2,32,8,1,128]{4,3,2,0,1:T(1,128)} %copy-done.5, ...), kind=kLoop, calls=%fused_computation.103 | loop fusion | flops 12058624 | bytes 10526720 | tf_op jit(solution)/shard_map/add | solution.py:93
  138.2 5.2 %collective-permute-start.7 = (f32[2,32,8,10,1]{1,2,4,3,0:T(8,128)S(1)}, f32[2,32,8,10,1]{1,2,4,3,0:T(8,128)}, u32[]{:S(2)}, u32[]{:S(2)}) collective-permute-start(f32[2,32,8,10,1]{1,2,4,3,0:T(8,128)S(1)} %copy.100), channel_id=1, source_target_pairs={{0,1},{1,2},{2,3},{4,5},{5,6},{6,7},{8,9},{9,10},{10,11},{12,13},{... | collective-permute-start | bytes 61448 | tf_op jit(solution)/shard_map/ppermute | solution.py:19
  152.3 5.3 %copy.101 = f32[2,32,8,10,1]{4,3,2,0,1:T(8,128)} copy(f32[2,32,8,10,1]{1,2,4,3,0:T(8,128)} %collective-permute-done.7) | data formatting | bytes 40960 | tf_op jit(solution)/shard_map/ppermute | solution.py:19
  157.6 5.2 %copy.99 = f32[2,32,8,10,1]{4,3,2,0,1:T(8,128)} copy(f32[2,32,8,10,1]{1,2,4,3,0:T(8,128)} %collective-permute-done.6) | data formatting | bytes 40960 | tf_op jit(solution)/shard_map/ppermute | solution.py:22
  162.8 8.1 %fusion.26 = f32[2,32,8,8,128]{4,3,2,0,1:T(8,128)S(1)} fusion(f32[1,32,8,8,128]{4,3,2,0,1:T(8,128)} %copy-done.2, f32[1,32,8,8,128]{4,3,2,0,1:T(8,128)S(1)} %get-tuple-element.20, f32[2,32,8,10,1]{4,3,2,0,1:T(8,128)} %copy.101, f32[2,32,8,1,128]{4,3,2,0,1:T(1,128)S(1)} %collective-permute-done.4, f32[2,32,8,1,128]{4,3,2,0,1:T(1,128)} %collective-permute-done.5, ...), kind=kLoop, calls=%fused_computation.81 | loop fusion | flops 12058624 | bytes 10526720 | tf_op jit(solution)/shard_map/add | solution.py:93
  179.3 12.4 %custom-call.9 = f32[4,32,32]{2,1,0:T(8,128)S(1)} custom-call(f32[4,32,32]{2,1,0:T(8,128)} %add_multiply_fusion.3), custom_call_target="Cholesky" | custom-call | tf_op jit(solution)/shard_map/jit(cholesky)/cholesky | solution.py:153
  202.6 5.2 %collective-permute-start.11 = (f32[2,32,8,10,1]{1,2,4,3,0:T(8,128)}, f32[2,32,8,10,1]{1,2,4,3,0:T(8,128)}, u32[]{:S(2)}, u32[]{:S(2)}) collective-permute-start(f32[2,32,8,10,1]{1,2,4,3,0:T(8,128)} %copy.104), channel_id=1, source_target_pairs={{0,1},{1,2},{2,3},{4,5},{5,6},{6,7},{8,9},{9,10},{10,11},{12,13},{... | collective-permute-start | bytes 61448 | tf_op jit(solution)/shard_map/ppermute | solution.py:19
  216.4 5.3 %copy.105 = f32[2,32,8,10,1]{4,3,2,0,1:T(8,128)} copy(f32[2,32,8,10,1]{1,2,4,3,0:T(8,128)} %collective-permute-done.11) | data formatting | bytes 40960 | tf_op jit(solution)/shard_map/ppermute | solution.py:19
  221.7 5.2 %copy.103 = f32[2,32,8,10,1]{4,3,2,0,1:T(8,128)} copy(f32[2,32,8,10,1]{1,2,4,3,0:T(8,128)} %collective-permute-done.10) | data formatting | bytes 40960 | tf_op jit(solution)/shard_map/ppermute | solution.py:22
  226.9 8.0 %fusion.18 = f32[2,32,8,8,128]{4,3,2,0,1:T(8,128)S(1)} fusion(f32[1,32,8,8,128]{4,3,2,0,1:T(8,128)} %copy-done.1, f32[1,32,8,8,128]{4,3,2,0,1:T(8,128)S(1)} %get-tuple-element.18, f32[2,32,8,10,1]{4,3,2,0,1:T(8,128)} %copy.105, f32[2,32,8,1,128]{4,3,2,0,1:T(1,128)S(1)} %collective-permute-done.8, f32[2,32,8,1,128]{4,3,2,0,1:T(1,128)} %collective-permute-done.9, ...), kind=kLoop, calls=%fused_computation.59 | loop fusion | flops 12058624 | bytes 10526720 | tf_op jit(solution)/shard_map/add | solution.py:93
  252.0 5.2 %collective-permute-start.15 = (f32[2,32,8,10,1]{1,2,4,3,0:T(8,128)}, f32[2,32,8,10,1]{1,2,4,3,0:T(8,128)}, u32[]{:S(2)}, u32[]{:S(2)}) collective-permute-start(f32[2,32,8,10,1]{1,2,4,3,0:T(8,128)} %copy.108), channel_id=1, source_target_pairs={{0,1},{1,2},{2,3},{4,5},{5,6},{6,7},{8,9},{9,10},{10,11},{12,13},{... | collective-permute-start | bytes 61448 | tf_op jit(solution)/shard_map/ppermute | solution.py:19
  264.5 5.3 %copy.109 = f32[2,32,8,10,1]{4,3,2,0,1:T(8,128)} copy(f32[2,32,8,10,1]{1,2,4,3,0:T(8,128)} %collective-permute-done.15) | data formatting | bytes 40960 | tf_op jit(solution)/shard_map/ppermute | solution.py:19
  269.8 5.2 %copy.107 = f32[2,32,8,10,1]{4,3,2,0,1:T(8,128)} copy(f32[2,32,8,10,1]{1,2,4,3,0:T(8,128)} %collective-permute-done.14) | data formatting | bytes 40960 | tf_op jit(solution)/shard_map/ppermute | solution.py:22
  275.0 7.4 %fusion.10 = f32[2,32,128]{2,0,1:T(2,128)S(1)} fusion(f32[1,32,8,8,128]{4,3,2,0,1:T(8,128)S(1)} %get-tuple-element.7, f32[1,32,8,8,128]{4,3,2,0,1:T(8,128)S(1)} %get-tuple-element.6, f32[2,32,8,10,1]{4,3,2,0,1:T(8,128)} %copy.109, f32[2,32,8,1,128]{4,3,2,0,1:T(1,128)S(1)} %collective-permute-done.12, f32[2,32,8,1,128]{4,3,2,0,1:T(1,128)} %copy-done.6, ...), kind=kLoop, calls=%fused_computation.37 | loop fusion | flops 13623296 | bytes 10559488 | tf_op jit(solution)/shard_map/reduce_sum | solution.py:113
  283.3 5.7 %all-to-all-start.1 = ((f32[32,2,4]{2,1,0:T(2,128)}), f32[32,2,4]{2,1,0:T(2,128)S(1)}, u32[]{:S(2)}, u32[]{:S(2)}) async-start(f32[32,2,4]{2,1,0:T(2,128)} %bitcast.18), calls=%async_computation.1 | async-start | bytes 65536 | tf_op jit(solution)/shard_map/all_to_all | solution.py:126
  289.2 9.8 %custom-call.10 = f32[4,1,32,32]{2,3,1,0:T(8,128)S(1)} custom-call(f32[4,1,32,32]{3,2,1,0:T(8,128)S(1)} %select_bitcast_fusion), custom_call_target="InvertDiagBlocksLowerTriangular" | custom-call | tf_op jit(solution)/shard_map/triangular_solve | solution.py:156
  299.6 10.6 %all_to_all.45 = f32[4,2,32]{0,1,2:T(2,128)S(1)} all-to-all(f32[4,2,32]{0,1,2:T(2,128)S(1)} %copy.114), channel_id=1, replica_groups=mesh['tm'=4,'sx'=2,'sy'=4] {'sx','sy'}, dimensions={2} | all-to-all | bytes 2048 | tf_op jit(solution)/shard_map/all_to_all | solution.py:160
  314.9 9.2 %reshape.398 = f32[2,32,8192]{2,0,1:T(2,128)} reshape(f32[2,32,8,1,8,4,32]{6,5,4,2,0,1,3:T(4,128)} %broadcast_in_dim.76) | data formatting | bytes 4194304 | tf_op jit(solution)/shard_map/reshape | solution.py:177
  328.6 85.0 %all-gather.5.cloned.1.call-done = f32[2,128,8192]{2,0,1:T(2,128)} async-done(((f32[2,32,8192]{2,0,1:T(2,128)}), f32[2,128,8192]{2,0,1:T(2,128)}) %all-gather.5.cloned.1.call-update) | async-done | bytes 8388624 | tf_op jit(solution)/shard_map/all_gather | solution.py:188
  413.5 11.1 %fusion.109 = (f32[1,128,8192]{2,0,1:T(1,128)S(1)}, f32[1,128,8192]{2,0,1:T(1,128)S(1)}) fusion(f32[2,128,8192]{2,0,1:T(2,128)} %all-gather.5.cloned.1.call-done), kind=kLoop, calls=%fused_computation.246 | loop fusion | bytes 16777216 | tf_op jit(solution)/shard_map/slice | solution.py:183
  (160 shorter events, 148.1 us)
Async XLA Ops:
  6.5 58.4 %all-gather.3.cloned.1.call-start = ((), (), s32[]{:S(2)}) async-start(), calls=%async_computation.3 | async-start | bytes 5242880 | tf_op jit(solution)/shard_map/all_gather | solution.py:71
  16.0 110.7 %all-to-all-start = ((f32[8,1,4]{2,1,0:T(1,128)}), f32[8,1,4]{2,1,0:T(1,128)}, u32[]{:S(2)}, u32[]{:S(2)}) async-start(f32[8,1,4]{2,1,0:T(1,128)} %broadcast_in_dim.75), calls=%async_computation | async-start | bytes 8192 | tf_op jit(solution)/shard_map/all_to_all | solution.py:127
  23.0 54.5 %copy-start.14 = (f32[32]{0:T(128)}, f32[32]{0:T(128)S(1)}, u32[]{:S(2)}) copy-start(f32[32]{0:T(128)S(1)} %cosine_subtract_fusion) | copy-start | bytes 388
  23.1 49.1 %copy-start.20 = (f32[32]{0:T(128)}, f32[32]{0:T(128)S(1)}, u32[]{:S(2)}) copy-start(f32[32]{0:T(128)S(1)} %get-tuple-element.53) | copy-start | bytes 388
  72.1 154.8 %copy-start = (f32[4,8,64,128]{3,2,1,0:T(8,128)}, f32[4,8,64,128]{3,2,1,0:T(8,128)S(1)}, u32[]{:S(2)}) copy-start(f32[4,8,64,128]{3,2,1,0:T(8,128)S(1)} %copy.127) | copy-start | bytes 3145732
  73.1 5.7 %collective-permute-start = (f32[2,32,8,1,128]{4,3,2,0,1:T(1,128)S(1)}, f32[2,32,8,1,128]{4,3,2,0,1:T(1,128)S(1)}, u32[]{:S(2)}, u32[]{:S(2)}) collective-permute-start(f32[2,32,8,1,128]{4,3,2,0,1:T(1,128)S(1)} %get-tuple-element.39), channel_id=1, source_target_pairs={{4,0},{5,1},{6,2},{7,3},{12,8},{13,9},{14,10},{15,11},{20,16},{21,... | collective-permute-start | bytes 786440 | tf_op jit(solution)/shard_map/ppermute | solution.py:22
  74.4 4.4 %collective-permute-start.1 = (f32[2,32,8,1,128]{4,3,2,0,1:T(1,128)S(1)}, f32[2,32,8,1,128]{4,3,2,0,1:T(1,128)S(1)}, u32[]{:S(2)}, u32[]{:S(2)}) collective-permute-start(f32[2,32,8,1,128]{4,3,2,0,1:T(1,128)S(1)} %get-tuple-element.38), channel_id=1, source_target_pairs={{0,4},{1,5},{2,6},{3,7},{8,12},{9,13},{10,14},{11,15},{16,20},{17,... | collective-permute-start | bytes 786440 | tf_op jit(solution)/shard_map/ppermute | solution.py:19
  87.7 12.8 %collective-permute-start.3 = (f32[2,32,8,10,1]{1,2,4,3,0:T(8,128)S(1)}, f32[2,32,8,10,1]{1,2,4,3,0:T(8,128)}, u32[]{:S(2)}, u32[]{:S(2)}) collective-permute-start(f32[2,32,8,10,1]{1,2,4,3,0:T(8,128)S(1)} %copy.96), channel_id=1, source_target_pairs={{0,1},{1,2},{2,3},{4,5},{5,6},{6,7},{8,9},{9,10},{10,11},{12,13},{... | collective-permute-start | bytes 61448 | tf_op jit(solution)/shard_map/ppermute | solution.py:19
  95.4 10.3 %collective-permute-start.2 = (f32[2,32,8,10,1]{1,2,4,3,0:T(8,128)}, f32[2,32,8,10,1]{1,2,4,3,0:T(8,128)}, u32[]{:S(2)}, u32[]{:S(2)}) collective-permute-start(f32[2,32,8,10,1]{1,2,4,3,0:T(8,128)} %copy.94), channel_id=1, source_target_pairs={{1,0},{2,1},{3,2},{5,4},{6,5},{7,6},{9,8},{10,9},{11,10},{13,12},{... | collective-permute-start | bytes 61448 | tf_op jit(solution)/shard_map/ppermute | solution.py:22
  121.7 6.5 %collective-permute-start.4 = (f32[2,32,8,1,128]{4,3,2,0,1:T(1,128)}, f32[2,32,8,1,128]{4,3,2,0,1:T(1,128)S(1)}, u32[]{:S(2)}, u32[]{:S(2)}) collective-permute-start(f32[2,32,8,1,128]{4,3,2,0,1:T(1,128)} %get-tuple-element.35), channel_id=1, source_target_pairs={{4,0},{5,1},{6,2},{7,3},{12,8},{13,9},{14,10},{15,11},{20,16},{21,... | collective-permute-start | bytes 786440 | tf_op jit(solution)/shard_map/ppermute | solution.py:22
  123.0 5.2 %collective-permute-start.5 = (f32[2,32,8,1,128]{4,3,2,0,1:T(1,128)}, f32[2,32,8,1,128]{4,3,2,0,1:T(1,128)}, u32[]{:S(2)}, u32[]{:S(2)}) collective-permute-start(f32[2,32,8,1,128]{4,3,2,0,1:T(1,128)} %get-tuple-element.34), channel_id=1, source_target_pairs={{0,4},{1,5},{2,6},{3,7},{8,12},{9,13},{10,14},{11,15},{16,20},{17,... | collective-permute-start | bytes 786440 | tf_op jit(solution)/shard_map/ppermute | solution.py:19
  138.2 14.1 %collective-permute-start.7 = (f32[2,32,8,10,1]{1,2,4,3,0:T(8,128)S(1)}, f32[2,32,8,10,1]{1,2,4,3,0:T(8,128)}, u32[]{:S(2)}, u32[]{:S(2)}) collective-permute-start(f32[2,32,8,10,1]{1,2,4,3,0:T(8,128)S(1)} %copy.100), channel_id=1, source_target_pairs={{0,1},{1,2},{2,3},{4,5},{5,6},{6,7},{8,9},{9,10},{10,11},{12,13},{... | collective-permute-start | bytes 61448 | tf_op jit(solution)/shard_map/ppermute | solution.py:19
  147.1 10.5 %collective-permute-start.6 = (f32[2,32,8,10,1]{1,2,4,3,0:T(8,128)}, f32[2,32,8,10,1]{1,2,4,3,0:T(8,128)}, u32[]{:S(2)}, u32[]{:S(2)}) collective-permute-start(f32[2,32,8,10,1]{1,2,4,3,0:T(8,128)} %copy.98), channel_id=1, source_target_pairs={{1,0},{2,1},{3,2},{5,4},{6,5},{7,6},{9,8},{10,9},{11,10},{13,12},{... | collective-permute-start | bytes 61448 | tf_op jit(solution)/shard_map/ppermute | solution.py:22
  173.6 18.3 %collective-permute-start.8 = (f32[2,32,8,1,128]{4,3,2,0,1:T(1,128)}, f32[2,32,8,1,128]{4,3,2,0,1:T(1,128)S(1)}, u32[]{:S(2)}, u32[]{:S(2)}) collective-permute-start(f32[2,32,8,1,128]{4,3,2,0,1:T(1,128)} %get-tuple-element.31), channel_id=1, source_target_pairs={{4,0},{5,1},{6,2},{7,3},{12,8},{13,9},{14,10},{15,11},{20,16},{21,... | collective-permute-start | bytes 786440 | tf_op jit(solution)/shard_map/ppermute | solution.py:22
  174.9 17.1 %collective-permute-start.9 = (f32[2,32,8,1,128]{4,3,2,0,1:T(1,128)}, f32[2,32,8,1,128]{4,3,2,0,1:T(1,128)}, u32[]{:S(2)}, u32[]{:S(2)}) collective-permute-start(f32[2,32,8,1,128]{4,3,2,0,1:T(1,128)} %get-tuple-element.30), channel_id=1, source_target_pairs={{0,4},{1,5},{2,6},{3,7},{8,12},{9,13},{10,14},{11,15},{16,20},{17,... | collective-permute-start | bytes 786440 | tf_op jit(solution)/shard_map/ppermute | solution.py:19
  202.6 13.9 %collective-permute-start.11 = (f32[2,32,8,10,1]{1,2,4,3,0:T(8,128)}, f32[2,32,8,10,1]{1,2,4,3,0:T(8,128)}, u32[]{:S(2)}, u32[]{:S(2)}) collective-permute-start(f32[2,32,8,10,1]{1,2,4,3,0:T(8,128)} %copy.104), channel_id=1, source_target_pairs={{0,1},{1,2},{2,3},{4,5},{5,6},{6,7},{8,9},{9,10},{10,11},{12,13},{... | collective-permute-start | bytes 61448 | tf_op jit(solution)/shard_map/ppermute | solution.py:19
  211.4 10.3 %collective-permute-start.10 = (f32[2,32,8,10,1]{1,2,4,3,0:T(8,128)}, f32[2,32,8,10,1]{1,2,4,3,0:T(8,128)}, u32[]{:S(2)}, u32[]{:S(2)}) collective-permute-start(f32[2,32,8,10,1]{1,2,4,3,0:T(8,128)} %copy.102), channel_id=1, source_target_pairs={{1,0},{2,1},{3,2},{5,4},{6,5},{7,6},{9,8},{10,9},{11,10},{13,12},{... | collective-permute-start | bytes 61448 | tf_op jit(solution)/shard_map/ppermute | solution.py:22
  237.0 5.6 %collective-permute-start.12 = (f32[2,32,8,1,128]{4,3,2,0,1:T(1,128)S(1)}, f32[2,32,8,1,128]{4,3,2,0,1:T(1,128)S(1)}, u32[]{:S(2)}, u32[]{:S(2)}) collective-permute-start(f32[2,32,8,1,128]{4,3,2,0,1:T(1,128)S(1)} %get-tuple-element.27), channel_id=1, source_target_pairs={{4,0},{5,1},{6,2},{7,3},{12,8},{13,9},{14,10},{15,11},{20,16},{21,... | collective-permute-start | bytes 786440 | tf_op jit(solution)/shard_map/ppermute | solution.py:22
  238.3 4.3 collective-permute-start.13
  252.0 12.4 %collective-permute-start.15 = (f32[2,32,8,10,1]{1,2,4,3,0:T(8,128)}, f32[2,32,8,10,1]{1,2,4,3,0:T(8,128)}, u32[]{:S(2)}, u32[]{:S(2)}) collective-permute-start(f32[2,32,8,10,1]{1,2,4,3,0:T(8,128)} %copy.108), channel_id=1, source_target_pairs={{0,1},{1,2},{2,3},{4,5},{5,6},{6,7},{8,9},{9,10},{10,11},{12,13},{... | collective-permute-start | bytes 61448 | tf_op jit(solution)/shard_map/ppermute | solution.py:19
  260.9 8.9 %collective-permute-start.14 = (f32[2,32,8,10,1]{1,2,4,3,0:T(8,128)}, f32[2,32,8,10,1]{1,2,4,3,0:T(8,128)}, u32[]{:S(2)}, u32[]{:S(2)}) collective-permute-start(f32[2,32,8,10,1]{1,2,4,3,0:T(8,128)} %copy.106), channel_id=1, source_target_pairs={{1,0},{2,1},{3,2},{5,4},{6,5},{7,6},{9,8},{10,9},{11,10},{13,12},{... | collective-permute-start | bytes 61448 | tf_op jit(solution)/shard_map/ppermute | solution.py:22
  283.3 15.7 %all-to-all-start.1 = ((f32[32,2,4]{2,1,0:T(2,128)}), f32[32,2,4]{2,1,0:T(2,128)S(1)}, u32[]{:S(2)}, u32[]{:S(2)}) async-start(f32[32,2,4]{2,1,0:T(2,128)} %bitcast.18), calls=%async_computation.1 | async-start | bytes 65536 | tf_op jit(solution)/shard_map/all_to_all | solution.py:126
  289.1 124.5 %all-gather.5.cloned.1.call-start = ((), (), s32[]{:S(2)}) async-start(), calls=%async_computation.4 | async-start | bytes 10485760 | tf_op jit(solution)/shard_map/all_gather | solution.py:188
  328.5 96.2 %copy-start.24 = (s32[32]{0:T(128)S(1)}, s32[32]{0:T(128)}, u32[]{:S(2)}) copy-start(s32[32]{0:T(128)} %copy-done.23) | copy-start | bytes 388
  (23 other events, 237.3 us)
Sparse Core Ops, SparseCore 0:
  9.5 55.3 all-gather.2
  328.7 84.8 all-gather.4
where the time goes:
time: 451 us; the launch traced here: 443 us
  waiting for transfers between devices  126 us (28%)
  local copies, waits for them, and re-layouts  123 us (27%)
  other arithmetic  95.7 us (21%)
  starting transfers between devices  56.5 us (13%)
  matrix products  16.5 us (4%)
  between operations  14.5 us (3%)
  blocking collectives  10.6 us (2%)
    all_gather x1, waiting for transfers between devices, local(): lax.all_gather(unrolled_array, 'tm', axis=1, tiled=True)  85 us
    all_gather x1, waiting for transfers between devices, local(): lax.all_gather(processor_lines, 'tm', axis=0, tiled=True)  40.7 us
    slice x8, local copies, waits for them, and re-layouts, extended(): lax.slice_in_dim(block, 0, width, axis=dim)  34.2 us
    ppermute x8, starting transfers between devices, extended(): lax.ppermute(lax.slice_in_dim(block, block.shape[dim] - width, None, axis...  33.2 us
    add x3, other arithmetic, local(): source_term + neighbors(present_guess)  24.1 us
    ppermute x4, local copies, waits for them, and re-layouts, extended(): lax.ppermute(lax.slice_in_dim(block, block.shape[dim] - width, None, axis...  21.1 us
    ppermute x4, local copies, waits for them, and re-layouts, extended(): lax.ppermute(lax.slice_in_dim(block, 0, width, axis=dim), axis, backward)  20.9 us
    dot_general x4, matrix products, matmul(): jnp.dot(left_side, right_side, precision=lax.Precision.HIGHEST, preferred...  16.1 us
  transfers between devices with their start and end apart: 20, of which 2 were waited for; matrix products, arithmetic and copies ran while one was open for 26% of the time, Pallas kernels for 0%

commit v1 on v0

--- a/solution.py
+++ b/solution.py
@@ -1,6 +1,11 @@
+import functools
+
 import jax
 import jax.numpy as jnp
+import numpy as np
 from jax import lax
+from jax.experimental import pallas as pl
+from jax.experimental.pallas import tpu as pltpu
 from jax.sharding import PartitionSpec as P
 
 AGGREGATE_XCELLS = 8
@@ -50,7 +55,7 @@
     return running
 
 
-def local(driving_input, regime, reaction_rates):
+def local_general(driving_input, regime, reaction_rates):
     moment_count, third_axis_count, first_axis_count, second_axis_count = driving_input.shape
     temporal_spacing = lax.axis_size("tm")
     sy_size = lax.axis_size("sy")
@@ -193,6 +198,542 @@
     return result.reshape(driving_input.shape)
 
 
+def time_tables(count):
+    half = count // 2
+    lane = np.arange(count)
+    frequency = np.where(lane <= half, lane, lane - half)
+    imaginary = lane > half
+    moment = np.arange(count)
+    angle = 2.0 * np.pi * (moment[:, None] * frequency[None, :] % count) / count
+    forward = np.where(imaginary[None, :], -np.sin(angle), np.cos(angle))
+    weight = np.where((lane == 0) | (lane == half), 1.0, 2.0) / count
+    theta = 2.0 * np.pi * frequency / count
+    signed = np.where(lane % half == 0, 0.0, np.sin(theta)) * np.where(lane < half, 1.0, -1.0)
+    shift = np.zeros((8, count))
+    shift[0] = 1.0 - np.cos(theta)
+    shift[1] = signed
+    return (
+        forward.astype(np.float32),
+        (forward * weight[None, :]).astype(np.float32),
+        shift.astype(np.float32),
+    )
+
+
+def fused_kernel(
+    sizes,
+    rates_ref,
+    field_ref,
+    regime_ref,
+    forward_ref,
+    backward_ref,
+    shift_ref,
+    out_ref,
+    send_buf,
+    recv_buf,
+    send_back,
+    recv_back,
+    cell_rates,
+    rate_tiles,
+    coarse_tiles,
+    weights,
+    source,
+    inv_real,
+    inv_cross,
+    iterate_0,
+    iterate_1,
+    iterate_2,
+    final,
+    there_send,
+    there_recv,
+    back_send,
+    back_recv,
+    rate_send,
+    rate_recv,
+    coarse_send,
+    coarse_recv,
+    halo_send,
+    halo_recv,
+):
+    teams, nsx, nsy, moments, nz, nx, lanes, width = sizes
+    total = teams * moments
+    half = total // 2
+    groups = nz // teams
+    chunk = moments * groups * nx
+    row_cells = width * nz
+    spatial = nsx * nsy
+    devices = teams * spatial
+    highest = lax.Precision.HIGHEST
+    tm = lax.axis_index("tm")
+    ix = lax.axis_index("sx")
+    iy = lax.axis_index("sy")
+    here = ix * nsy + iy
+    me = tm * spatial + here
+
+    def place(rank):
+        return {
+            "tm": rank // spatial,
+            "sx": (rank % spatial) // nsy,
+            "sy": rank % nsy,
+        }
+
+    barrier = pltpu.get_barrier_semaphore()
+
+    def greet(offset, carry):
+        pl.semaphore_signal(
+            barrier,
+            inc=1,
+            device_id=place((me + offset) % devices),
+            device_id_type=pl.DeviceIdType.MESH,
+        )
+        return carry
+
+    lax.fori_loop(1, devices, greet, 0)
+
+    rates = jnp.zeros(regime_ref.shape, jnp.float32)
+    regime = regime_ref[...]
+    for number in range(rates_ref.shape[0]):
+        rates = rates + jnp.where(regime == number, rates_ref[number], 0.0)
+    cell_rates[...] = rates.reshape(nz * nx, lanes)
+    rate_tiles[here] = jnp.sum(rates, axis=0)
+
+    lane_block = lax.broadcasted_iota(jnp.int32, (1, nx, lanes), 2) // width
+
+    def swap(parts):
+        result = []
+        for target in range(teams):
+            merged = parts[target]
+            for other in range(teams):
+                if other != target:
+                    turn = (width * (other - target)) % lanes
+                    merged = jnp.where(
+                        lane_block == other, pltpu.roll(parts[other], turn, 2), merged
+                    )
+            result.append(merged)
+        return result
+
+    step = 2
+
+    def pack(index, carry):
+        first = index * step
+        for group in range(groups):
+            parts = swap(
+                [field_ref[pl.ds(first, step), group * teams + j] for j in range(teams)]
+            )
+            for target in range(teams):
+                for inner in range(step):
+                    row = target * chunk + ((first + inner) * groups + group) * nx
+                    send_buf[pl.ds(pl.multiple_of(row, nx), nx), :] = parts[target][inner]
+        return carry
+
+    lax.fori_loop(0, moments // step, pack, 0)
+    pl.semaphore_wait(barrier, devices - 1)
+
+    def chunk_of(ref, index):
+        return ref.at[pl.ds(pl.multiple_of(index * chunk, chunk), chunk), :]
+
+    def there(offset):
+        peer = (tm + offset) % teams
+        return pltpu.make_async_remote_copy(
+            src_ref=chunk_of(send_buf, peer),
+            dst_ref=chunk_of(recv_buf, tm),
+            send_sem=there_send.at[offset],
+            recv_sem=there_recv.at[offset],
+            device_id={"tm": peer, "sx": ix, "sy": iy},
+            device_id_type=pl.DeviceIdType.MESH,
+        )
+
+    def rate_copy(offset):
+        peer = (here + offset) % spatial
+        return pltpu.make_async_remote_copy(
+            src_ref=rate_tiles.at[here],
+            dst_ref=rate_tiles.at[here],
+            send_sem=rate_send.at[offset],
+            recv_sem=rate_recv.at[offset],
+            device_id={"tm": tm, "sx": peer // nsy, "sy": peer % nsy},
+            device_id_type=pl.DeviceIdType.MESH,
+        )
+
+    for offset in range(1, spatial):
+        rate_copy(offset).start()
+    for offset in range(1, teams):
+        there(offset).start()
+    recv_buf[pl.ds(pl.multiple_of(tm * chunk, chunk), chunk), :] = send_buf[
+        pl.ds(pl.multiple_of(tm * chunk, chunk), chunk), :
+    ]
+
+    shift_real = shift_ref[0:1, :]
+    shift_cross = shift_ref[1:2, :]
+
+    def divisors(x, carry):
+        rows = cell_rates[pl.ds(x, nz, stride=nx), :]
+        rows = pltpu.roll(rows, ((teams - tm) * width) % lanes, 1)
+        for y in range(width):
+            diag = jnp.broadcast_to(rows[:, y : y + 1], (nz, total)) + 6.0 + shift_real
+            inverse = 1.0 / (diag * diag + shift_cross * shift_cross)
+            at = pl.ds(pl.multiple_of(x * row_cells + y * nz, nz), nz)
+            inv_real[at, :] = diag * inverse
+            inv_cross[at, :] = shift_cross * inverse
+        return carry
+
+    lax.fori_loop(0, nx, divisors, 0)
+
+    ncy = nsy * teams
+    for offset in range(1, spatial):
+        rate_copy(offset).wait()
+    strip_block = lax.broadcasted_iota(jnp.int32, (nx, lanes), 1) // width
+    faces = 2 * (width * nz + nx * nz)
+    couple_x = -float(width * nz)
+    couple_y = -float(nx * nz)
+    unknowns = ncy * nsx
+    band = [[None] * (nsx + 1) for _ in range(unknowns)]
+    right = []
+    own = (iy * teams + tm) * nsx + ix
+    for gy in range(ncy):
+        for gx in range(nsx):
+            number = gy * nsx + gx
+            tile = rate_tiles[gx * nsy + gy // teams]
+            amount = jnp.sum(jnp.where(strip_block == gy % teams, tile, 0.0), axis=0, keepdims=True)
+            amount = jnp.sum(amount, axis=1, keepdims=True)
+            band[number][0] = amount + faces + float(nx * width * nz) * shift_real
+            if gx + 1 < nsx:
+                band[number][1] = jnp.full((1, total), couple_x, jnp.float32)
+            if gy + 1 < ncy:
+                extra = jnp.full((1, total), couple_y, jnp.float32)
+                before = band[number][nsx]
+                band[number][nsx] = extra if before is None else before + extra
+            right.append(jnp.where(own == number, jnp.ones((1, total), jnp.float32), 0.0))
+    inverses = []
+    for i in range(unknowns):
+        inverse = 1.0 / band[i][0]
+        inverses.append(inverse)
+        for a in range(1, nsx + 1):
+            if band[i][a] is None or i + a >= unknowns:
+                continue
+            ratio = band[i][a] * inverse
+            right[i + a] = right[i + a] - ratio * right[i]
+            for b in range(a, nsx + 1):
+                if band[i][b] is None or i + b >= unknowns:
+                    continue
+                term = ratio * band[i][b]
+                before = band[i + a][b - a]
+                band[i + a][b - a] = -term if before is None else before - term
+    row_solution = [None] * unknowns
+    for i in reversed(range(unknowns)):
+        value = right[i]
+        for a in range(1, nsx + 1):
+            if i + a < unknowns and band[i][a] is not None:
+                value = value - band[i][a] * row_solution[i + a]
+        row_solution[i] = value * inverses[i]
+    zero_row = jnp.zeros((1, total), jnp.float32)
+
+    def weight(gx, gy):
+        inside = 0 <= gx < nsx and 0 <= gy < ncy
+        return row_solution[gy * nsx + gx] if inside else zero_row
+
+    for gy in range(ncy):
+        for gx in range(nsx):
+            slot = (gy % teams) * spatial + gx * nsy + gy // teams
+            weights[slot] = jnp.concatenate(
+                [
+                    weight(gx, gy),
+                    weight(gx - 1, gy),
+                    weight(gx + 1, gy),
+                    weight(gx, gy - 1),
+                    weight(gx, gy + 1),
+                    zero_row,
+                    zero_row,
+                    zero_row,
+                ],
+                axis=0,
+            )
+
+    strip = iy * teams + tm
+    has = (ix > 0, ix < nsx - 1, strip > 0, strip < ncy - 1)
+
+    def strip_place(rank):
+        return {"tm": rank % teams, "sx": ix, "sy": rank // teams}
+
+    neighbour = (
+        {"tm": tm, "sx": (ix + nsx - 1) % nsx, "sy": iy},
+        {"tm": tm, "sx": (ix + 1) % nsx, "sy": iy},
+        strip_place((strip + ncy - 1) % ncy),
+        strip_place((strip + 1) % ncy),
+    )
+    xs, ys = pl.ds(1, nx), pl.ds(1, width)
+    iterates = (iterate_0, iterate_1, iterate_2)
+
+    def layers(ref):
+        edges = (ref.at[1, ys], ref.at[nx, ys], ref.at[xs, 1], ref.at[xs, width])
+        halos = (ref.at[0, ys], ref.at[nx + 1, ys], ref.at[xs, 0], ref.at[xs, width + 1])
+        return edges, halos
+
+    for ref in iterates:
+        _, halos = layers(ref)
+        for side in range(4):
+
+            @pl.when(jnp.logical_not(has[side]))
+            def _(halo=halos[side]):
+                halo[...] = jnp.zeros(halo.shape, jnp.float32)
+
+    def halo_copies(number):
+        edges, halos = layers(iterates[number])
+        return [
+            pltpu.make_async_remote_copy(
+                src_ref=edges[side],
+                dst_ref=halos[side ^ 1],
+                send_sem=halo_send.at[number * 4 + side],
+                recv_sem=halo_recv.at[number * 4 + (side ^ 1)],
+                device_id=neighbour[side],
+                device_id_type=pl.DeviceIdType.MESH,
+            )
+            for side in range(4)
+        ]
+
+    def exchange(number):
+        copies = halo_copies(number)
+        for side in range(4):
+
+            @pl.when(has[side])
+            def _(copy=copies[side]):
+                copy.start()
+
+        for side in range(4):
+
+            @pl.when(has[side])
+            def _(side=side):
+                copies[side].wait_send()
+                copies[side ^ 1].wait_recv()
+
+    def divide(x, values):
+        at = pl.ds(pl.multiple_of(x * row_cells, row_cells), row_cells)
+        turned = pltpu.roll(values, half, 1)
+        return inv_real[at, :] * values + inv_cross[at, :] * turned
+
+    for offset in range(1, teams):
+        there(offset).wait()
+
+    def transform(x, carry):
+        for group in range(groups):
+            block = recv_buf[pl.ds(group * nx + x, total, stride=groups * nx), :]
+            block = lax.dot_general(
+                block,
+                forward_ref[...],
+                (((0,), (0,)), ((), ())),
+                precision=highest,
+                preferred_element_type=jnp.float32,
+            )
+            for j in range(teams):
+                z = group * teams + j
+                source[pl.ds(x * row_cells + z, width, stride=nz), :] = block[
+                    j * width : (j + 1) * width
+                ]
+        at = pl.ds(pl.multiple_of(x * row_cells, row_cells), row_cells)
+        iterate_0[x + 1, ys] = divide(x, source[at, :]).reshape(width, nz, total)
+        return carry
+
+    lax.fori_loop(0, nx, transform, 0)
+
+    def sweep(old, x):
+        middle = old[x + 1, ys]
+        running = old[x, ys] + old[x + 2, ys]
+        running = running + old[x + 1, pl.ds(0, width)] + old[x + 1, pl.ds(2, width)]
+        running = running + pltpu.roll(middle, 1, 1) + pltpu.roll(middle, nz - 1, 1)
+        at = pl.ds(pl.multiple_of(x * row_cells, row_cells), row_cells)
+        return divide(x, source[at, :] + running.reshape(row_cells, total))
+
+    for number in range(2):
+        exchange(number)
+
+        def advance(x, carry, old=iterates[number], new=iterates[number + 1]):
+            new[x + 1, ys] = sweep(old, x).reshape(width, nz, total)
+            return carry
+
+        lax.fori_loop(0, nx, advance, 0)
+    exchange(2)
+
+    def finish(x, carry):
+        sums, weighted, sources, low_y, high_y = carry
+        values = sweep(iterate_2, x)
+        at = pl.ds(pl.multiple_of(x * row_cells, row_cells), row_cells)
+        final[at, :] = values
+        cells = values.reshape(width, nz, total)
+        rows = cell_rates[pl.ds(x, nz, stride=nx), :]
+        rows = pltpu.roll(rows, ((teams - tm) * width) % lanes, 1)
+        for y in range(width):
+            weighted = weighted + cells[y] * rows[:, y : y + 1]
+        sources = sources + jnp.sum(source[at, :].reshape(width, nz, total), axis=0)
+        layer = jnp.sum(cells, axis=0)
+        return sums + layer, weighted, sources, low_y + cells[0], high_y + cells[width - 1]
+
+    blank = jnp.zeros((nz, total), jnp.float32)
+    sums, weighted, sources, low_y, high_y = lax.fori_loop(
+        0, nx, finish, (blank, blank, blank, blank, blank)
+    )
+    layer_rows = width * nz
+    low_x = jnp.sum(final[0:layer_rows, :].reshape(width, nz, total), axis=0)
+    high_x = jnp.sum(
+        final[(nx - 1) * layer_rows : nx * layer_rows, :].reshape(width, nz, total), axis=0
+    )
+    balance = sources - weighted - shift_real * sums + shift_cross * pltpu.roll(sums, half, 1)
+    balance = balance - low_x - high_x - low_y - high_y
+    coarse_tiles[me] = jnp.concatenate(
+        [
+            jnp.sum(part, axis=0, keepdims=True)
+            for part in (balance, low_x, high_x, low_y, high_y)
+        ]
+        + [zero_row] * 3,
+        axis=0,
+    )
+
+    def coarse_copy(offset):
+        return pltpu.make_async_remote_copy(
+            src_ref=coarse_tiles.at[me],
+            dst_ref=coarse_tiles.at[me],
+            send_sem=coarse_send.at[offset],
+            recv_sem=coarse_recv.at[offset],
+            device_id=place((me + offset) % devices),
+            device_id_type=pl.DeviceIdType.MESH,
+        )
+
+    def coarse_start(offset, carry):
+        coarse_copy(offset).start()
+        return carry
+
+    def coarse_wait(offset, carry):
+        coarse_copy(offset).wait()
+        return carry
+
+    lax.fori_loop(1, devices, coarse_start, 0)
+    lax.fori_loop(1, devices, coarse_wait, 0)
+    correction = jnp.sum(coarse_tiles[...] * weights[...], axis=0)
+    correction = jnp.sum(correction, axis=0, keepdims=True)
+
+    def restore(x, carry):
+        for group in range(groups):
+            block = jnp.concatenate(
+                [
+                    final[pl.ds(x * row_cells + group * teams + j, width, stride=nz), :]
+                    for j in range(teams)
+                ],
+                axis=0,
+            )
+            block = lax.dot_general(
+                backward_ref[...],
+                block + correction,
+                (((1,), (1,)), ((), ())),
+                precision=highest,
+                preferred_element_type=jnp.float32,
+            )
+            send_back[pl.ds(group * nx + x, total, stride=groups * nx), :] = block
+        return carry
+
+    lax.fori_loop(0, nx, restore, 0)
+
+    def back(offset):
+        peer = (tm + offset) % teams
+        return pltpu.make_async_remote_copy(
+            src_ref=chunk_of(send_back, peer),
+            dst_ref=chunk_of(recv_back, tm),
+            send_sem=back_send.at[offset],
+            recv_sem=back_recv.at[offset],
+            device_id={"tm": peer, "sx": ix, "sy": iy},
+            device_id_type=pl.DeviceIdType.MESH,
+        )
+
+    for offset in range(1, teams):
+        back(offset).start()
+    recv_back[pl.ds(pl.multiple_of(tm * chunk, chunk), chunk), :] = send_back[
+        pl.ds(pl.multiple_of(tm * chunk, chunk), chunk), :
+    ]
+    for offset in range(1, teams):
+        back(offset).wait()
+
+    def unpack(index, carry):
+        first = index * step
+        for group in range(groups):
+            parts = []
+            for origin in range(teams):
+                rows = []
+                for inner in range(step):
+                    row = origin * chunk + ((first + inner) * groups + group) * nx
+                    rows.append(recv_back[pl.ds(pl.multiple_of(row, nx), nx), :])
+                parts.append(jnp.stack(rows))
+            parts = swap(parts)
+            for j in range(teams):
+                out_ref[pl.ds(first, step), group * teams + j] = parts[j]
+        return carry
+
+    lax.fori_loop(0, moments // step, unpack, 0)
+
+
+def local_fused(teams, nsx, nsy, driving_input, regime, reaction_rates):
+    moments, nz, nx, lanes = driving_input.shape
+    width = lanes // teams
+    total = teams * moments
+    forward, backward, shift = time_tables(total)
+    sizes = (teams, nsx, nsy, moments, nz, nx, lanes, width)
+    cells = nx * width * nz
+    devices = teams * nsx * nsy
+    rows = total * (nz // teams) * nx
+    f32 = jnp.float32
+    padded = pltpu.VMEM((nx + 2, width + 2, nz, total), f32)
+    vmem = pl.BlockSpec(memory_space=pltpu.VMEM)
+    dma = pltpu.SemaphoreType.DMA
+    return pl.pallas_call(
+        functools.partial(fused_kernel, sizes),
+        out_shape=jax.ShapeDtypeStruct(driving_input.shape, f32),
+        in_specs=[pl.BlockSpec(memory_space=pltpu.SMEM)] + [vmem] * 5,
+        out_specs=vmem,
+        scratch_shapes=[
+            pltpu.VMEM((rows, lanes), f32),
+            pltpu.VMEM((rows, lanes), f32),
+            pltpu.VMEM((rows, lanes), f32),
+            pltpu.VMEM((rows, lanes), f32),
+            pltpu.VMEM((nz * nx, lanes), f32),
+            pltpu.VMEM((nsx * nsy, nx, lanes), f32),
+            pltpu.VMEM((devices, 8, total), f32),
+            pltpu.VMEM((devices, 8, total), f32),
+            pltpu.VMEM((cells, total), f32),
+            pltpu.VMEM((cells, total), f32),
+            pltpu.VMEM((cells, total), f32),
+            padded,
+            padded,
+            padded,
+            pltpu.VMEM((cells, total), f32),
+            dma((teams,)),
+            dma((teams,)),
+            dma((teams,)),
+            dma((teams,)),
+            dma((nsx * nsy,)),
+            dma((nsx * nsy,)),
+            dma((devices,)),
+            dma((devices,)),
+            dma((12,)),
+            dma((12,)),
+        ],
+        compiler_params=pltpu.CompilerParams(
+            collective_id=0, has_side_effects=True, vmem_limit_bytes=48 * 1024 * 1024
+        ),
+    )(
+        reaction_rates,
+        driving_input,
+        regime,
+        jnp.asarray(forward),
+        jnp.asarray(backward),
+        jnp.asarray(shift),
+    )
+
+
+def local(driving_input, regime, reaction_rates):
+    moments, nz, nx, lanes = driving_input.shape
+    teams, nsx, nsy = (lax.axis_size(axis) for axis in ("tm", "sx", "sy"))
+    one_aggregate = nx == AGGREGATE_XCELLS and lanes == teams * AGGREGATE_YCELLS
+    tiled = nx == 8 and nz == 8 and nz % teams == 0 and lanes == 128
+    if one_aggregate and tiled and teams * moments == 128 and SWEEPS == 4:
+        return local_fused(teams, nsx, nsy, driving_input, regime, reaction_rates)
+    return local_general(driving_input, regime, reaction_rates)
+
+
 def solution(mesh):
     placed = (P("tm", None, "sx", "sy"), P(None, "sx", "sy"), P())
     return jax.shard_map(

time: 451 us -> 69.9 us (0.15); the launches traced: 443 us -> 69.5 us
  waiting for transfers between devices: 126 us -> 0 us
  local copies, waits for them, and re-layouts: 123 us -> 5.97 us
  other arithmetic: 95.7 us -> 0 us
  Pallas kernels: 0 us -> 63.6 us
  starting transfers between devices: 56.5 us -> 0 us
  matrix products: 16.5 us -> 0 us
  between operations: 14.5 us -> 0.02 us
  blocking collectives: 10.6 us -> 0 us
    all_gather x2 -> x0, waiting for transfers between devices: 126 us -> none  [the longest x1 85 us: local(): lax.all_gather(unrolled_array, 'tm', axis=1, tiled=True)]
    pallas_call x0 -> x1, Pallas kernels: none -> 63.6 us  [local_fused(): pl.pallas_call(functools.partial(fused_kernel, sizes), out_shape=jax.Shap...]
    slice x14 -> x0, local copies, waits for them, and re-layouts: 59.7 us -> none  [the longest x8 34.2 us: extended(): lax.slice_in_dim(block, 0, width, axis=dim)]
    ppermute x16 -> x0, starting transfers between devices: 44.4 us -> none  [the longest x8 33.2 us: extended(): lax.ppermute(lax.slice_in_dim(block, block.shape[dim] - width, None, axis...]
    ppermute x8 -> x0, local copies, waits for them, and re-layouts: 42 us -> none  [the longest x4 21.1 us: extended(): lax.ppermute(lax.slice_in_dim(block, block.shape[dim] - width, None, axis...]
    another operation x11 -> x0, other arithmetic: 36.4 us -> none  [the longest x4 13.2 us: local(): factor = jnp.linalg.cholesky(system)]
    add x9 -> x0, other arithmetic: 31.2 us -> none  [the longest x3 24.1 us: local(): source_term + neighbors(present_guess)]
    dot_general x4 -> x0, matrix products: 16.1 us -> none  [matmul(): jnp.dot(left_side, right_side, precision=lax.Precision.HIGHEST, preferred...]
  transfers between devices with their start and end apart: 20 -> 0, of which waited for: 2 -> 0; matrix products, arithmetic and copies ran while one was open for 26% -> 0% of each run, Pallas kernels for 0% -> 0%
where the time goes in v1:
time: 69.9 us; the launch traced here: 69.5 us
  Pallas kernels  63.6 us (91%)
  local copies, waits for them, and re-layouts  5.97 us (9%)
    pallas_call x1, Pallas kernels, local_fused(): pl.pallas_call(functools.partial(fused_kernel, sizes), out_shape=jax.Shap...  63.6 us
    unnamed x13, local copies, waits for them, and re-layouts  5.97 us

profile of v1, /device:TPU:0, one launch (start us, length us, event | category | flops | bytes accessed | tf_op | source)
XLA Modules:
  0.0 69.5 jit_solution(16247026406992394465)
XLA Ops:
  0.0 0.0 copy-start
  0.0 1.2 %copy-done = f32[32,8,8,128]{3,2,1,0:T(8,128)S(1)} copy-done((f32[32,8,8,128]{3,2,1,0:T(8,128)S(1)}, f32[32,8,8,128]{3,2,1,0:T(8,128)}, u32[]{:S(2)}) %copy-start) | copy-done | bytes 1048600
  1.2 0.0 copy-start.1
  1.2 0.8 %copy-done.1 = f32[128,128]{1,0:T(8,128)S(1)} copy-done((f32[128,128]{1,0:T(8,128)S(1)}, f32[128,128]{1,0:T(8,128)}, u32[]{:S(2)}) %copy-start.1) | copy-done | bytes 65560
  2.1 0.0 copy-start.2
  2.1 0.8 %copy-done.2 = f32[128,128]{1,0:T(8,128)S(1)} copy-done((f32[128,128]{1,0:T(8,128)S(1)}, f32[128,128]{1,0:T(8,128)}, u32[]{:S(2)}) %copy-start.2) | copy-done | bytes 65560
  2.9 0.0 copy-start.3
  2.9 0.8 %copy-done.3 = s32[8,8,128]{2,1,0:T(8,128)S(1)} copy-done((s32[8,8,128]{2,1,0:T(8,128)S(1)}, s32[8,8,128]{2,1,0:T(8,128)}, u32[]{:S(2)}) %copy-start.3) | copy-done | bytes 32792
  3.7 0.0 copy-start.4
  3.7 0.7 copy-done.4
  4.4 0.0 copy-start.5
  4.4 0.7 copy-done.5
  5.0 63.6 %shard_map.64 = f32[32,8,8,128]{3,2,1,0:T(8,128)S(1)} custom-call(f32[8]{0:T(128)S(1)} %copy-done.5, f32[32,8,8,128]{3,2,1,0:T(8,128)S(1)} %copy-done, s32[8,8,128]{2,1,0:T(8,128)S(1)} %copy-done.3, f32[128,128]{1,0:T(8,128)S(1)} %copy-done.2, f32[128,128]{1,0:T(8,128)S(1)} %copy-done.1, f32[8,128]{1,0:T(8,128)S(1)} %copy-done.4), custom_call_target="tpu_custom_call" | custom-call | tf_op jit(solution)/shard_map/pallas_call | solution.py:682
  68.6 1.0 %copy.8 = f32[32,8,8,128]{3,2,1,0:T(8,128)} copy(f32[32,8,8,128]{3,2,1,0:T(8,128)S(1)} %shard_map.64) | data formatting | bytes 2097152
Async XLA Ops:
  0.0 1.2 %copy-start = (f32[32,8,8,128]{3,2,1,0:T(8,128)S(1)}, f32[32,8,8,128]{3,2,1,0:T(8,128)}, u32[]{:S(2)}) copy-start(f32[32,8,8,128]{3,2,1,0:T(8,128)} %field_ref.1) | copy-start | bytes 3145732
  1.2 0.8 %copy-start.1 = (f32[128,128]{1,0:T(8,128)S(1)}, f32[128,128]{1,0:T(8,128)}, u32[]{:S(2)}) copy-start(f32[128,128]{1,0:T(8,128)} %constant.7.clone.backward_ref) | copy-start | bytes 196612
  2.1 0.8 %copy-start.2 = (f32[128,128]{1,0:T(8,128)S(1)}, f32[128,128]{1,0:T(8,128)}, u32[]{:S(2)}) copy-start(f32[128,128]{1,0:T(8,128)} %constant.6.clone.forward_ref) | copy-start | bytes 196612
  2.9 0.8 %copy-start.3 = (s32[8,8,128]{2,1,0:T(8,128)S(1)}, s32[8,8,128]{2,1,0:T(8,128)}, u32[]{:S(2)}) copy-start(s32[8,8,128]{2,1,0:T(8,128)} %regime_ref.1) | copy-start | bytes 98308
  3.7 0.7 copy-start.4
  4.4 0.7 copy-start.5

commit v2 on v1

--- a/solution.py
+++ b/solution.py
@@ -212,21 +212,19 @@
     shift = np.zeros((8, count))
     shift[0] = 1.0 - np.cos(theta)
     shift[1] = signed
-    return (
-        forward.astype(np.float32),
-        (forward * weight[None, :]).astype(np.float32),
-        shift.astype(np.float32),
-    )
+    return np.concatenate([forward, forward * weight[None, :], shift]).astype(np.float32)
 
 
 def fused_kernel(
     sizes,
     rates_ref,
+    field_hbm,
+    regime_hbm,
+    table_hbm,
+    out_hbm,
     field_ref,
     regime_ref,
-    forward_ref,
-    backward_ref,
-    shift_ref,
+    table_ref,
     out_ref,
     send_buf,
     recv_buf,
@@ -235,7 +233,8 @@
     cell_rates,
     rate_tiles,
     coarse_tiles,
-    weights,
+    solved_tiles,
+    shifts,
     source,
     inv_real,
     inv_cross,
@@ -243,6 +242,8 @@
     iterate_1,
     iterate_2,
     final,
+    load_sem,
+    store_sem,
     there_send,
     there_recv,
     back_send,
@@ -258,7 +259,7 @@
     total = teams * moments
     half = total // 2
     groups = nz // teams
-    chunk = moments * groups * nx
+    piece = moments * nx
     row_cells = width * nz
     spatial = nsx * nsy
     devices = teams * spatial
@@ -269,6 +270,20 @@
     here = ix * nsy + iy
     me = tm * spatial + here
 
+    def group_part(ref, group):
+        return ref.at[:, pl.ds(group * teams, teams)]
+
+    loads = [
+        pltpu.make_async_copy(
+            group_part(field_hbm, group), group_part(field_ref, group), load_sem.at[group]
+        )
+        for group in range(groups)
+    ]
+    loads.append(pltpu.make_async_copy(regime_hbm, regime_ref, load_sem.at[groups]))
+    loads.append(pltpu.make_async_copy(table_hbm, table_ref, load_sem.at[groups + 1]))
+    for load in loads:
+        load.start()
+
     def place(rank):
         return {
             "tm": rank // spatial,
@@ -289,16 +304,25 @@
 
     lax.fori_loop(1, devices, greet, 0)
 
-    rates = jnp.zeros(regime_ref.shape, jnp.float32)
-    regime = regime_ref[...]
-    for number in range(rates_ref.shape[0]):
-        rates = rates + jnp.where(regime == number, rates_ref[number], 0.0)
-    cell_rates[...] = rates.reshape(nz * nx, lanes)
-    rate_tiles[here] = jnp.sum(rates, axis=0)
-
     lane_block = lax.broadcasted_iota(jnp.int32, (1, nx, lanes), 2) // width
 
     def swap(parts):
+        if teams & (teams - 1) == 0:
+            bit = teams // 2
+            while bit:
+                upper = lane_block & bit != 0
+                result = list(parts)
+                for low in range(teams):
+                    if low & bit:
+                        continue
+                    first, second = parts[low], parts[low | bit]
+                    result[low] = jnp.where(upper, pltpu.roll(second, width * bit, 2), first)
+                    result[low | bit] = jnp.where(
+                        upper, second, pltpu.roll(first, lanes - width * bit, 2)
+                    )
+                parts = result
+                bit //= 2
+            return parts
         result = []
         for target in range(teams):
             merged = parts[target]
@@ -311,36 +335,66 @@
             result.append(merged)
         return result
 
-    step = 2
-
-    def pack(index, carry):
-        first = index * step
-        for group in range(groups):
+    step = 4
+
+    def row_at(group, origin, moment):
+        return pl.ds(
+            pl.multiple_of((group * teams + origin) * piece + moment * nx, nx), step * nx
+        )
+
+    def pack(group):
+        def body(index, carry):
+            first = index * step
             parts = swap(
                 [field_ref[pl.ds(first, step), group * teams + j] for j in range(teams)]
             )
             for target in range(teams):
-                for inner in range(step):
-                    row = target * chunk + ((first + inner) * groups + group) * nx
-                    send_buf[pl.ds(pl.multiple_of(row, nx), nx), :] = parts[target][inner]
-        return carry
-
-    lax.fori_loop(0, moments // step, pack, 0)
-    pl.semaphore_wait(barrier, devices - 1)
-
-    def chunk_of(ref, index):
-        return ref.at[pl.ds(pl.multiple_of(index * chunk, chunk), chunk), :]
-
-    def there(offset):
+                send_buf[row_at(group, target, first), :] = parts[target].reshape(
+                    step * nx, lanes
+                )
+            return carry
+
+        lax.fori_loop(0, moments // step, body, 0)
+
+    def piece_of(ref, group, index):
+        return ref.at[pl.ds(pl.multiple_of((group * teams + index) * piece, piece), piece), :]
+
+    def over_teams(source_buf, target_buf, send_sem, recv_sem, group, offset):
         peer = (tm + offset) % teams
         return pltpu.make_async_remote_copy(
-            src_ref=chunk_of(send_buf, peer),
-            dst_ref=chunk_of(recv_buf, tm),
-            send_sem=there_send.at[offset],
-            recv_sem=there_recv.at[offset],
+            src_ref=piece_of(source_buf, group, peer),
+            dst_ref=piece_of(target_buf, group, tm),
+            send_sem=send_sem.at[group * teams + offset],
+            recv_sem=recv_sem.at[group * teams + offset],
             device_id={"tm": peer, "sx": ix, "sy": iy},
             device_id_type=pl.DeviceIdType.MESH,
         )
+
+    def there(group, offset):
+        return over_teams(send_buf, recv_buf, there_send, there_recv, group, offset)
+
+    def back(group, offset):
+        return over_teams(send_back, recv_back, back_send, back_recv, group, offset)
+
+    def keep(source_buf, target_buf, group):
+        at = pl.ds(pl.multiple_of((group * teams + tm) * piece, piece), piece)
+        target_buf[at, :] = source_buf[at, :]
+
+    for group in range(groups):
+        loads[group].wait()
+        pack(group)
+        if group == 0:
+            pl.semaphore_wait(barrier, devices - 1)
+        for offset in range(1, teams):
+            there(group, offset).start()
+
+    loads[groups].wait()
+    rates = jnp.zeros(regime_ref.shape, jnp.float32)
+    regime = regime_ref[...]
+    for number in range(rates_ref.shape[0]):
+        rates = rates + jnp.where(regime == number, rates_ref[number], 0.0)
+    cell_rates[...] = rates.reshape(nz * nx, lanes)
+    rate_tiles[here] = jnp.sum(rates, axis=0)
 
     def rate_copy(offset):
         peer = (here + offset) % spatial
@@ -355,14 +409,12 @@
 
     for offset in range(1, spatial):
         rate_copy(offset).start()
-    for offset in range(1, teams):
-        there(offset).start()
-    recv_buf[pl.ds(pl.multiple_of(tm * chunk, chunk), chunk), :] = send_buf[
-        pl.ds(pl.multiple_of(tm * chunk, chunk), chunk), :
-    ]
-
-    shift_real = shift_ref[0:1, :]
-    shift_cross = shift_ref[1:2, :]
+    for group in range(groups):
+        keep(send_buf, recv_buf, group)
+    loads[groups + 1].wait()
+
+    shift_real = table_ref[2 * total : 2 * total + 1, :]
+    shift_cross = table_ref[2 * total + 1 : 2 * total + 2, :]
 
     def divisors(x, carry):
         rows = cell_rates[pl.ds(x, nz, stride=nx), :]
@@ -386,8 +438,6 @@
     couple_y = -float(nx * nz)
     unknowns = ncy * nsx
     band = [[None] * (nsx + 1) for _ in range(unknowns)]
-    right = []
-    own = (iy * teams + tm) * nsx + ix
     for gy in range(ncy):
         for gx in range(nsx):
             number = gy * nsx + gx
@@ -401,51 +451,23 @@
                 extra = jnp.full((1, total), couple_y, jnp.float32)
                 before = band[number][nsx]
                 band[number][nsx] = extra if before is None else before + extra
-            right.append(jnp.where(own == number, jnp.ones((1, total), jnp.float32), 0.0))
     inverses = []
+    ratios = []
     for i in range(unknowns):
         inverse = 1.0 / band[i][0]
         inverses.append(inverse)
+        ratios.append([None] * (nsx + 1))
         for a in range(1, nsx + 1):
             if band[i][a] is None or i + a >= unknowns:
                 continue
             ratio = band[i][a] * inverse
-            right[i + a] = right[i + a] - ratio * right[i]
+            ratios[i][a] = ratio
             for b in range(a, nsx + 1):
                 if band[i][b] is None or i + b >= unknowns:
                     continue
                 term = ratio * band[i][b]
                 before = band[i + a][b - a]
                 band[i + a][b - a] = -term if before is None else before - term
-    row_solution = [None] * unknowns
-    for i in reversed(range(unknowns)):
-        value = right[i]
-        for a in range(1, nsx + 1):
-            if i + a < unknowns and band[i][a] is not None:
-                value = value - band[i][a] * row_solution[i + a]
-        row_solution[i] = value * inverses[i]
-    zero_row = jnp.zeros((1, total), jnp.float32)
-
-    def weight(gx, gy):
-        inside = 0 <= gx < nsx and 0 <= gy < ncy
-        return row_solution[gy * nsx + gx] if inside else zero_row
-
-    for gy in range(ncy):
-        for gx in range(nsx):
-            slot = (gy % teams) * spatial + gx * nsy + gy // teams
-            weights[slot] = jnp.concatenate(
-                [
-                    weight(gx, gy),
-                    weight(gx - 1, gy),
-                    weight(gx + 1, gy),
-                    weight(gx, gy - 1),
-                    weight(gx, gy + 1),
-                    zero_row,
-                    zero_row,
-                    zero_row,
-                ],
-                axis=0,
-            )
 
     strip = iy * teams + tm
     has = (ix > 0, ix < nsx - 1, strip > 0, strip < ncy - 1)
@@ -475,7 +497,7 @@
             def _(halo=halos[side]):
                 halo[...] = jnp.zeros(halo.shape, jnp.float32)
 
-    def halo_copies(number):
+    def halo_copies(number, sides):
         edges, halos = layers(iterates[number])
         return [
             pltpu.make_async_remote_copy(
@@ -486,17 +508,18 @@
                 device_id=neighbour[side],
                 device_id_type=pl.DeviceIdType.MESH,
             )
-            for side in range(4)
+            for side in sides
         ]
 
-    def exchange(number):
-        copies = halo_copies(number)
-        for side in range(4):
+    def exchange_start(number, sides):
+        for side, copy in zip(sides, halo_copies(number, sides)):
 
             @pl.when(has[side])
-            def _(copy=copies[side]):
+            def _(copy=copy):
                 copy.start()
 
+    def exchange_wait(number):
+        copies = halo_copies(number, range(4))
         for side in range(4):
 
             @pl.when(has[side])
@@ -504,20 +527,59 @@
                 copies[side].wait_send()
                 copies[side ^ 1].wait_recv()
 
-    def divide(x, values):
-        at = pl.ds(pl.multiple_of(x * row_cells, row_cells), row_cells)
+    def cells_at(x, first, count):
+        return pl.ds(pl.multiple_of(x * row_cells + first * nz, nz), count * nz)
+
+    def divide(at, values):
         turned = pltpu.roll(values, half, 1)
         return inv_real[at, :] * values + inv_cross[at, :] * turned
 
-    for offset in range(1, teams):
-        there(offset).wait()
-
-    def transform(x, carry):
-        for group in range(groups):
-            block = recv_buf[pl.ds(group * nx + x, total, stride=groups * nx), :]
+    def sweep(old, x, first, count):
+        middle = old[x + 1, pl.ds(first + 1, count)]
+        running = old[x, pl.ds(first + 1, count)] + old[x + 2, pl.ds(first + 1, count)]
+        running = running + old[x + 1, pl.ds(first, count)]
+        running = running + old[x + 1, pl.ds(first + 2, count)]
+        running = running + pltpu.roll(middle, 1, 1) + pltpu.roll(middle, nz - 1, 1)
+        at = cells_at(x, first, count)
+        return divide(at, source[at, :] + running.reshape(count * nz, total))
+
+    def update(number, x, first, count):
+        at = cells_at(x, first, count)
+        if number == 0:
+            values = divide(at, source[at, :])
+        else:
+            values = sweep(iterates[number - 1], x, first, count)
+        iterates[number][x + 1, pl.ds(first + 1, count)] = values.reshape(count, nz, total)
+
+    def advance(number):
+        if number:
+            exchange_wait(number - 1)
+        update(number, 0, 0, width)
+        update(number, nx - 1, 0, width)
+        exchange_start(number, (0, 1))
+
+        def edge(x, carry):
+            update(number, x, 0, 1)
+            update(number, x, width - 1, 1)
+            return carry
+
+        def inner(x, carry):
+            update(number, x, 1, width - 2)
+            return carry
+
+        lax.fori_loop(1, nx - 1, edge, 0, unroll=True)
+        exchange_start(number, (2, 3))
+        lax.fori_loop(1, nx - 1, inner, 0)
+
+    for group in range(groups):
+        for offset in range(1, teams):
+            there(group, offset).wait()
+
+        def transform(x, carry, group=group):
+            block = recv_buf[pl.ds(group * teams * piece + x, total, stride=nx), :]
             block = lax.dot_general(
                 block,
-                forward_ref[...],
+                table_ref[0:total, :],
                 (((0,), (0,)), ((), ())),
                 precision=highest,
                 preferred_element_type=jnp.float32,
@@ -527,55 +589,28 @@
                 source[pl.ds(x * row_cells + z, width, stride=nz), :] = block[
                     j * width : (j + 1) * width
                 ]
-        at = pl.ds(pl.multiple_of(x * row_cells, row_cells), row_cells)
-        iterate_0[x + 1, ys] = divide(x, source[at, :]).reshape(width, nz, total)
-        return carry
-
-    lax.fori_loop(0, nx, transform, 0)
-
-    def sweep(old, x):
-        middle = old[x + 1, ys]
-        running = old[x, ys] + old[x + 2, ys]
-        running = running + old[x + 1, pl.ds(0, width)] + old[x + 1, pl.ds(2, width)]
-        running = running + pltpu.roll(middle, 1, 1) + pltpu.roll(middle, nz - 1, 1)
-        at = pl.ds(pl.multiple_of(x * row_cells, row_cells), row_cells)
-        return divide(x, source[at, :] + running.reshape(row_cells, total))
-
-    for number in range(2):
-        exchange(number)
-
-        def advance(x, carry, old=iterates[number], new=iterates[number + 1]):
-            new[x + 1, ys] = sweep(old, x).reshape(width, nz, total)
             return carry
 
-        lax.fori_loop(0, nx, advance, 0)
-    exchange(2)
+        lax.fori_loop(0, nx, transform, 0, unroll=4)
+
+    for number in range(3):
+        advance(number)
+    exchange_wait(2)
 
     def finish(x, carry):
-        sums, weighted, sources, low_y, high_y = carry
-        values = sweep(iterate_2, x)
-        at = pl.ds(pl.multiple_of(x * row_cells, row_cells), row_cells)
-        final[at, :] = values
-        cells = values.reshape(width, nz, total)
-        rows = cell_rates[pl.ds(x, nz, stride=nx), :]
-        rows = pltpu.roll(rows, ((teams - tm) * width) % lanes, 1)
-        for y in range(width):
-            weighted = weighted + cells[y] * rows[:, y : y + 1]
-        sources = sources + jnp.sum(source[at, :].reshape(width, nz, total), axis=0)
-        layer = jnp.sum(cells, axis=0)
-        return sums + layer, weighted, sources, low_y + cells[0], high_y + cells[width - 1]
+        sums, low_y, high_y = carry
+        values = sweep(iterate_2, x, 0, width)
+        final[cells_at(x, 0, width), :] = values
+        change = values.reshape(width, nz, total) - iterate_2[x + 1, ys]
+        layer = jnp.sum(change, axis=0)
+        shifts[x] = layer
+        return sums + layer, low_y + change[0], high_y + change[width - 1]
 
     blank = jnp.zeros((nz, total), jnp.float32)
-    sums, weighted, sources, low_y, high_y = lax.fori_loop(
-        0, nx, finish, (blank, blank, blank, blank, blank)
-    )
-    layer_rows = width * nz
-    low_x = jnp.sum(final[0:layer_rows, :].reshape(width, nz, total), axis=0)
-    high_x = jnp.sum(
-        final[(nx - 1) * layer_rows : nx * layer_rows, :].reshape(width, nz, total), axis=0
-    )
-    balance = sources - weighted - shift_real * sums + shift_cross * pltpu.roll(sums, half, 1)
-    balance = balance - low_x - high_x - low_y - high_y
+    sums, low_y, high_y = lax.fori_loop(0, nx, finish, (blank, blank, blank))
+    low_x, high_x = shifts[0], shifts[nx - 1]
+    balance = 6.0 * sums - low_x - high_x - low_y - high_y
+    zero_row = jnp.zeros((1, total), jnp.float32)
     coarse_tiles[me] = jnp.concatenate(
         [
             jnp.sum(part, axis=0, keepdims=True)
@@ -603,13 +638,9 @@
         coarse_copy(offset).wait()
         return carry
 
-    lax.fori_loop(1, devices, coarse_start, 0)
-    lax.fori_loop(1, devices, coarse_wait, 0)
-    correction = jnp.sum(coarse_tiles[...] * weights[...], axis=0)
-    correction = jnp.sum(correction, axis=0, keepdims=True)
-
-    def restore(x, carry):
-        for group in range(groups):
+    for group in range(groups):
+
+        def restore(x, carry, group=group):
             block = jnp.concatenate(
                 [
                     final[pl.ds(x * row_cells + group * teams + j, width, stride=nz), :]
@@ -618,73 +649,130 @@
                 axis=0,
             )
             block = lax.dot_general(
-                backward_ref[...],
-                block + correction,
+                table_ref[total : 2 * total, :],
+                block,
                 (((1,), (1,)), ((), ())),
                 precision=highest,
                 preferred_element_type=jnp.float32,
             )
-            send_back[pl.ds(group * nx + x, total, stride=groups * nx), :] = block
-        return carry
-
-    lax.fori_loop(0, nx, restore, 0)
-
-    def back(offset):
-        peer = (tm + offset) % teams
-        return pltpu.make_async_remote_copy(
-            src_ref=chunk_of(send_back, peer),
-            dst_ref=chunk_of(recv_back, tm),
-            send_sem=back_send.at[offset],
-            recv_sem=back_recv.at[offset],
-            device_id={"tm": peer, "sx": ix, "sy": iy},
-            device_id_type=pl.DeviceIdType.MESH,
-        )
-
-    for offset in range(1, teams):
-        back(offset).start()
-    recv_back[pl.ds(pl.multiple_of(tm * chunk, chunk), chunk), :] = send_back[
-        pl.ds(pl.multiple_of(tm * chunk, chunk), chunk), :
-    ]
-    for offset in range(1, teams):
-        back(offset).wait()
-
-    def unpack(index, carry):
-        first = index * step
-        for group in range(groups):
-            parts = []
-            for origin in range(teams):
-                rows = []
-                for inner in range(step):
-                    row = origin * chunk + ((first + inner) * groups + group) * nx
-                    rows.append(recv_back[pl.ds(pl.multiple_of(row, nx), nx), :])
-                parts.append(jnp.stack(rows))
-            parts = swap(parts)
-            for j in range(teams):
-                out_ref[pl.ds(first, step), group * teams + j] = parts[j]
-        return carry
-
-    lax.fori_loop(0, moments // step, unpack, 0)
+            send_back[pl.ds(group * teams * piece + x, total, stride=nx), :] = block
+            return carry
+
+        lax.fori_loop(0, nx, restore, 0, unroll=4)
+        for offset in range(1, teams):
+            back(group, offset).start()
+        if group == 0:
+            lax.fori_loop(1, devices, coarse_start, 0)
+
+    for group in range(groups):
+        keep(send_back, recv_back, group)
+    lax.fori_loop(1, devices, coarse_wait, 0)
+
+    def coarse_row(gx, gy, row):
+        if not (0 <= gx < nsx and 0 <= gy < ncy):
+            return zero_row
+        slot = (gy % teams) * spatial + gx * nsy + gy // teams
+        return coarse_tiles[slot, row : row + 1, :]
+
+    right = []
+    for gy in range(ncy):
+        for gx in range(nsx):
+            right.append(
+                coarse_row(gx, gy, 0)
+                + coarse_row(gx + 1, gy, 1)
+                + coarse_row(gx - 1, gy, 2)
+                + coarse_row(gx, gy + 1, 3)
+                + coarse_row(gx, gy - 1, 4)
+            )
+    for i in range(unknowns):
+        for a in range(1, nsx + 1):
+            if ratios[i][a] is not None:
+                right[i + a] = right[i + a] - ratios[i][a] * right[i]
+    for i in reversed(range(unknowns)):
+        value = right[i] * inverses[i]
+        for a in range(1, nsx + 1):
+            if ratios[i][a] is not None:
+                value = value - ratios[i][a] * right[i + a]
+        right[i] = value
+    for gx in range(nsx):
+        for block in range(nsy):
+            for d in range(teams):
+                number = (block * teams + d) * nsx + gx
+                solved_tiles[gx * nsy + block, d : d + 1, :] = right[number]
+    own_rows = solved_tiles[here]
+    spread = jnp.concatenate(
+        [jnp.broadcast_to(own_rows[d : d + 1], (width, total)) for d in range(teams)], axis=0
+    )
+    own_moments = pl.ds(pl.multiple_of(total + tm * moments, moments), moments)
+    shifts[0:moments // nx] = lax.dot_general(
+        table_ref[own_moments, :],
+        spread,
+        (((1,), (1,)), ((), ())),
+        precision=highest,
+        preferred_element_type=jnp.float32,
+    ).reshape(moments // nx, nx, lanes)
+
+    stores = []
+    for group in range(groups):
+        for offset in range(1, teams):
+            back(group, offset).wait()
+
+        def unpack(index, carry, group=group):
+            first = index * nx
+            added = shifts[index]
+            for inner in range(0, nx, step):
+                parts = swap(
+                    [
+                        recv_back[row_at(group, origin, first + inner), :].reshape(
+                            step, nx, lanes
+                        )
+                        for origin in range(teams)
+                    ]
+                )
+                amount = jnp.stack(
+                    [
+                        jnp.broadcast_to(added[k : k + 1], (nx, lanes))
+                        for k in range(inner, inner + step)
+                    ]
+                )
+                for j in range(teams):
+                    out_ref[pl.ds(first + inner, step), group * teams + j] = parts[j] + amount
+            return carry
+
+        lax.fori_loop(0, moments // nx, unpack, 0)
+        store = pltpu.make_async_copy(
+            group_part(out_ref, group), group_part(out_hbm, group), store_sem.at[group]
+        )
+        store.start()
+        stores.append(store)
+    for store in stores:
+        store.wait()
 
 
 def local_fused(teams, nsx, nsy, driving_input, regime, reaction_rates):
     moments, nz, nx, lanes = driving_input.shape
     width = lanes // teams
     total = teams * moments
-    forward, backward, shift = time_tables(total)
+    table = time_tables(total)
     sizes = (teams, nsx, nsy, moments, nz, nx, lanes, width)
     cells = nx * width * nz
     devices = teams * nsx * nsy
-    rows = total * (nz // teams) * nx
+    groups = nz // teams
+    rows = total * groups * nx
     f32 = jnp.float32
     padded = pltpu.VMEM((nx + 2, width + 2, nz, total), f32)
-    vmem = pl.BlockSpec(memory_space=pltpu.VMEM)
+    in_place = pl.BlockSpec(memory_space=pl.ANY)
     dma = pltpu.SemaphoreType.DMA
     return pl.pallas_call(
         functools.partial(fused_kernel, sizes),
         out_shape=jax.ShapeDtypeStruct(driving_input.shape, f32),
-        in_specs=[pl.BlockSpec(memory_space=pltpu.SMEM)] + [vmem] * 5,
-        out_specs=vmem,
+        in_specs=[pl.BlockSpec(memory_space=pltpu.SMEM)] + [in_place] * 3,
+        out_specs=in_place,
         scratch_shapes=[
+            pltpu.VMEM(driving_input.shape, f32),
+            pltpu.VMEM(regime.shape, jnp.int32),
+            pltpu.VMEM(table.shape, f32),
+            pltpu.VMEM(driving_input.shape, f32),
             pltpu.VMEM((rows, lanes), f32),
             pltpu.VMEM((rows, lanes), f32),
             pltpu.VMEM((rows, lanes), f32),
@@ -692,7 +780,8 @@
             pltpu.VMEM((nz * nx, lanes), f32),
             pltpu.VMEM((nsx * nsy, nx, lanes), f32),
             pltpu.VMEM((devices, 8, total), f32),
-            pltpu.VMEM((devices, 8, total), f32),
+            pltpu.VMEM((nsx * nsy, max(teams, 8), total), f32),
+            pltpu.VMEM((max(nx, moments // nx), 8, total), f32),
             pltpu.VMEM((cells, total), f32),
             pltpu.VMEM((cells, total), f32),
             pltpu.VMEM((cells, total), f32),
@@ -700,10 +789,12 @@
             padded,
             padded,
             pltpu.VMEM((cells, total), f32),
-            dma((teams,)),
-            dma((teams,)),
-            dma((teams,)),
-            dma((teams,)),
+            dma((groups + 2,)),
+            dma((groups,)),
+            dma((groups * teams,)),
+            dma((groups * teams,)),
+            dma((groups * teams,)),
+            dma((groups * teams,)),
             dma((nsx * nsy,)),
             dma((nsx * nsy,)),
             dma((devices,)),
@@ -712,16 +803,9 @@
             dma((12,)),
         ],
         compiler_params=pltpu.CompilerParams(
-            collective_id=0, has_side_effects=True, vmem_limit_bytes=48 * 1024 * 1024
+            collective_id=0, has_side_effects=True, vmem_limit_bytes=60 * 1024 * 1024
         ),
-    )(
-        reaction_rates,
-        driving_input,
-        regime,
-        jnp.asarray(forward),
-        jnp.asarray(backward),
-        jnp.asarray(shift),
-    )
+    )(reaction_rates, driving_input, regime, jnp.asarray(table))
 
 
 def local(driving_input, regime, reaction_rates):
@@ -729,7 +813,7 @@
     teams, nsx, nsy = (lax.axis_size(axis) for axis in ("tm", "sx", "sy"))
     one_aggregate = nx == AGGREGATE_XCELLS and lanes == teams * AGGREGATE_YCELLS
     tiled = nx == 8 and nz == 8 and nz % teams == 0 and lanes == 128
-    if one_aggregate and tiled and teams * moments == 128 and SWEEPS == 4:
+    if one_aggregate and tiled and teams * moments == 128 and moments % 8 == 0 and SWEEPS == 4:
         return local_fused(teams, nsx, nsy, driving_input, regime, reaction_rates)
     return local_general(driving_input, regime, reaction_rates)
 

time: 69.9 us -> 53.6 us (0.77)
  Pallas kernels: 63.6 us -> 51.1 us
  local copies, waits for them, and re-layouts: 5.97 us -> 2.31 us
    pallas_call x1, Pallas kernels: 63.6 us -> 51.1 us  [local_fused(): pl.pallas_call(functools.partial(fused_kernel, sizes), out_shape=jax.Shap...]
    unnamed x13 -> x1, local copies, waits for them, and re-layouts: 5.97 us -> 2.31 us
where the time goes in v2:
time: 53.6 us; the launch traced here: 53.4 us
  Pallas kernels  51.1 us (95%)
  local copies, waits for them, and re-layouts  2.31 us (4%)
    pallas_call x1, Pallas kernels, local_fused(): pl.pallas_call(functools.partial(fused_kernel, sizes), out_shape=jax.Shap...  51.1 us
    unnamed x1, local copies, waits for them, and re-layouts  2.31 us

profile of v2, /device:TPU:0, one launch (start us, length us, event | category | flops | bytes accessed | tf_op | source)
XLA Modules:
  0.0 53.4 jit_solution(1512506705974251961)
XLA Ops:
  0.0 51.1 %shard_map.46 = f32[32,8,8,128]{3,2,1,0:T(8,128)} custom-call(f32[8]{0:T(128)} %rates_ref.1, f32[32,8,8,128]{3,2,1,0:T(8,128)} %field_hbm.1, s32[8,8,128]{2,1,0:T(8,128)} %regime_hbm.1, f32[264,128]{1,0:T(8,128)} %constant.2.clone.table_hbm), custom_call_target="tpu_custom_call" | custom-call | tf_op jit(solution)/shard_map/pallas_call | solution.py:766
  51.1 2.3 %copy.6 = f32[32,8,8,128]{3,2,1,0:T(8,128)} copy(f32[32,8,8,128]{3,2,1,0:T(8,128)} %shard_map.46) | data formatting | bytes 2097152

commit v3 on v0

--- a/solution.py
+++ b/solution.py
@@ -1,6 +1,11 @@
+import functools
+
 import jax
 import jax.numpy as jnp
+import numpy as np
 from jax import lax
+from jax.experimental import pallas as pl
+from jax.experimental.pallas import tpu as pltpu
 from jax.sharding import PartitionSpec as P
 
 AGGREGATE_XCELLS = 8
@@ -50,7 +55,7 @@
     return running
 
 
-def local(driving_input, regime, reaction_rates):
+def local_general(driving_input, regime, reaction_rates):
     moment_count, third_axis_count, first_axis_count, second_axis_count = driving_input.shape
     temporal_spacing = lax.axis_size("tm")
     sy_size = lax.axis_size("sy")
@@ -193,6 +198,526 @@
     return result.reshape(driving_input.shape)
 
 
+def time_tables(count):
+    half = count // 2
+    lane = np.arange(count)
+    frequency = np.where(lane <= half, lane, lane - half)
+    imaginary = lane > half
+    moment = np.arange(count)
+    angle = 2.0 * np.pi * (moment[:, None] * frequency[None, :] % count) / count
+    forward = np.where(imaginary[None, :], -np.sin(angle), np.cos(angle))
+    weight = np.where((lane == 0) | (lane == half), 1.0, 2.0) / count
+    theta = 2.0 * np.pi * frequency / count
+    signed = np.where(lane % half == 0, 0.0, np.sin(theta)) * np.where(lane < half, 1.0, -1.0)
+    shift = np.zeros((8, count))
+    shift[0] = 1.0 - np.cos(theta)
+    shift[1] = signed
+    return np.concatenate([forward, forward * weight[None, :], shift]).astype(np.float32)
+
+
+def fused_kernel(
+    sizes,
+    rates_ref,
+    field_hbm,
+    regime_hbm,
+    table_hbm,
+    out_ref,
+    field_ref,
+    regime_ref,
+    table_ref,
+    rate_tiles,
+    coarse_tiles,
+    solved_tiles,
+    added_ref,
+    layer_sums,
+    iterate_0,
+    iterate_1,
+    iterate_2,
+    iterate_3,
+    lasts,
+    x_edges,
+    x_halos,
+    y_edges,
+    y_halos,
+    load_sem,
+    last_send,
+    last_recv,
+    rate_send,
+    rate_recv,
+    coarse_send,
+    coarse_recv,
+    halo_send,
+    halo_recv,
+):
+    teams, nsx, nsy, moments, nz, nx, lanes, width = sizes
+    total = teams * moments
+    strips = lanes // width
+    plane = nz * nx
+    spatial = nsx * nsy
+    devices = teams * spatial
+    highest = lax.Precision.HIGHEST
+    tm = lax.axis_index("tm")
+    ix = lax.axis_index("sx")
+    iy = lax.axis_index("sy")
+    here = ix * nsy + iy
+    me = tm * spatial + here
+
+    loads = [
+        pltpu.make_async_copy(regime_hbm, regime_ref, load_sem.at[0]),
+        pltpu.make_async_copy(field_hbm, field_ref, load_sem.at[1]),
+        pltpu.make_async_copy(table_hbm, table_ref, load_sem.at[2]),
+    ]
+    for load in loads:
+        load.start()
+
+    def place(rank):
+        return {
+            "tm": rank // spatial,
+            "sx": (rank % spatial) // nsy,
+            "sy": rank % nsy,
+        }
+
+    barrier = pltpu.get_barrier_semaphore()
+
+    def greet(offset, carry):
+        pl.semaphore_signal(
+            barrier,
+            inc=1,
+            device_id=place((me + offset) % devices),
+            device_id_type=pl.DeviceIdType.MESH,
+        )
+        return carry
+
+    lax.fori_loop(1, devices, greet, 0)
+
+    loads[0].wait()
+    rates = jnp.zeros(regime_ref.shape, jnp.float32)
+    regime = regime_ref[...]
+    for number in range(rates_ref.shape[0]):
+        rates = rates + jnp.where(regime == number, rates_ref[number], 0.0)
+    rate_tiles[here] = jnp.sum(rates, axis=0)
+    decay = 1.0 / (rates + 7.0)
+    decay_block = jnp.ones_like(decay)
+    power, left = decay, moments
+    while left:
+        if left & 1:
+            decay_block = decay_block * power
+        power = power * power
+        left //= 2
+    decay_round = jnp.ones_like(decay)
+    for _ in range(teams):
+        decay_round = decay_round * decay_block
+    closing = 1.0 / (1.0 - decay_round)
+
+    has = (ix > 0, ix < nsx - 1, iy > 0, iy < nsy - 1)
+    neighbour = (
+        {"tm": tm, "sx": (ix + nsx - 1) % nsx, "sy": iy},
+        {"tm": tm, "sx": (ix + 1) % nsx, "sy": iy},
+        {"tm": tm, "sx": ix, "sy": (iy + nsy - 1) % nsy},
+        {"tm": tm, "sx": ix, "sy": (iy + 1) % nsy},
+    )
+    for number in range(3):
+        for side in range(4):
+
+            @pl.when(jnp.logical_not(has[side]))
+            def _(halo=(x_halos if side < 2 else y_halos).at[number, side % 2]):
+                halo[...] = jnp.zeros(halo.shape, jnp.float32)
+
+    def halo_copies(number):
+        copies = []
+        for side in range(4):
+            if side < 2:
+                source = x_edges.at[number, side]
+                target = x_halos.at[number, 1 - side]
+            else:
+                source = y_edges.at[number]
+                target = y_halos.at[number, 3 - side]
+            copies.append(
+                pltpu.make_async_remote_copy(
+                    src_ref=source,
+                    dst_ref=target,
+                    send_sem=halo_send.at[number * 4 + side],
+                    recv_sem=halo_recv.at[number * 4 + (side ^ 1)],
+                    device_id=neighbour[side],
+                    device_id_type=pl.DeviceIdType.MESH,
+                )
+            )
+        return copies
+
+    def exchange_start(number):
+        for side, copy in enumerate(halo_copies(number)):
+
+            @pl.when(has[side])
+            def _(copy=copy):
+                copy.start()
+
+    def exchange_wait(number):
+        copies = halo_copies(number)
+        for side in range(4):
+
+            @pl.when(has[side])
+            def _(side=side):
+                copies[side].wait_send()
+                copies[side ^ 1].wait_recv()
+
+    def rate_copy(offset):
+        peer = (here + offset) % spatial
+        return pltpu.make_async_remote_copy(
+            src_ref=rate_tiles.at[here],
+            dst_ref=rate_tiles.at[here],
+            send_sem=rate_send.at[offset],
+            recv_sem=rate_recv.at[offset],
+            device_id={"tm": tm, "sx": peer // nsy, "sy": peer % nsy},
+            device_id_type=pl.DeviceIdType.MESH,
+        )
+
+    def last_copy(number, offset):
+        return pltpu.make_async_remote_copy(
+            src_ref=lasts.at[number, tm],
+            dst_ref=lasts.at[number, tm],
+            send_sem=last_send.at[number * teams + offset],
+            recv_sem=last_recv.at[number * teams + offset],
+            device_id={"tm": (tm + offset) % teams, "sx": ix, "sy": iy},
+            device_id_type=pl.DeviceIdType.MESH,
+        )
+
+    iterates = (iterate_0, iterate_1, iterate_2, iterate_3)
+    chunk = lanes // 2 // nz
+    row_id = lax.broadcasted_iota(jnp.int32, (nx, lanes), 0)
+    lane_id = lax.broadcasted_iota(jnp.int32, (nx, lanes), 1)
+    first_row, last_row = row_id == 0, row_id == nx - 1
+    first_lane, last_lane = lane_id == 0, lane_id == lanes - 1
+    odd_lane = lane_id % 2 == 1
+    pair = (lane_id + 1) % lanes // 2
+
+    def recurrence(number):
+        def body(block, state):
+            if number:
+                high = y_halos[number - 1, 1, block]
+                low = pltpu.roll(y_halos[number - 1, 0, block], 2, 1)
+                ends = jnp.where(odd_lane, low, high)
+                old = iterates[number - 1]
+            state = list(state)
+            for inner in range(chunk):
+                moment = block * chunk + inner
+                if number:
+                    cells = [old[moment, z] for z in range(nz)]
+                for z in range(nz):
+                    values = field_ref[moment, z]
+                    if number:
+                        here_cell = cells[z]
+                        slot = inner * nz + z
+                        turned = pltpu.roll(ends, (lanes - 2 * slot - 1) % lanes, 1)
+                        row = moment * nz + z
+                        low_row = x_halos[number - 1, 0, pl.ds(row, 1), :]
+                        high_row = x_halos[number - 1, 1, pl.ds(row, 1), :]
+                        values = values + cells[z - 1] + cells[(z + 1) % nz]
+                        values = values + jnp.where(
+                            first_row, low_row, pltpu.roll(here_cell, 1, 0)
+                        )
+                        values = values + jnp.where(
+                            last_row, high_row, pltpu.roll(here_cell, nx - 1, 0)
+                        )
+                        values = values + jnp.where(
+                            first_lane, turned, pltpu.roll(here_cell, 1, 1)
+                        )
+                        values = values + jnp.where(
+                            last_lane, turned, pltpu.roll(here_cell, lanes - 1, 1)
+                        )
+                    state[z] = decay[z] * (values + state[z])
+                    iterates[number][moment, z] = state[z]
+            return tuple(state)
+
+        start = tuple(jnp.zeros((nx, lanes), jnp.float32) for _ in range(nz))
+        state = lax.fori_loop(0, moments // chunk, body, start)
+        for z in range(nz):
+            lasts[number, tm, z] = state[z]
+
+    def history(number):
+        value = lasts[number, tm]
+        for offset in range(1, teams):
+            value = lasts[number, (tm + offset) % teams] + decay_block * value
+        return value * closing
+
+    def complete(number, entry):
+        def body(block, state):
+            state = list(state)
+            packed = jnp.zeros((nx, lanes), jnp.float32)
+            for inner in range(chunk):
+                moment = block * chunk + inner
+                for z in range(nz):
+                    state[z] = decay[z] * state[z]
+                    values = iterates[number][moment, z] + state[z]
+                    iterates[number][moment, z] = values
+                    slot = inner * nz + z
+                    packed = jnp.where(pair == slot, pltpu.roll(values, 2 * slot, 1), packed)
+                    row = moment * nz + z
+                    x_edges[number, 0, pl.ds(row, 1), :] = values[0:1]
+                    x_edges[number, 1, pl.ds(row, 1), :] = values[nx - 1 : nx]
+            y_edges[number, block] = packed
+            return tuple(state)
+
+        lax.fori_loop(0, moments // chunk, body, tuple(entry[z] for z in range(nz)))
+
+    loads[1].wait()
+    recurrence(0)
+    pl.semaphore_wait(barrier, devices - 1)
+    for offset in range(1, teams):
+        last_copy(0, offset).start()
+    for offset in range(1, spatial):
+        rate_copy(offset).start()
+    for offset in range(1, teams):
+        last_copy(0, offset).wait()
+    complete(0, history(0))
+    exchange_start(0)
+
+    for offset in range(1, spatial):
+        rate_copy(offset).wait()
+    loads[2].wait()
+    shift_real = table_ref[2 * total : 2 * total + 1, :]
+    ncy = nsy * strips
+    strip_block = lax.broadcasted_iota(jnp.int32, (nx, lanes), 1) // width
+    faces = 2 * (width * nz + nx * nz)
+    couple_x = -float(width * nz)
+    couple_y = -float(nx * nz)
+    unknowns = ncy * nsx
+    band = [[None] * (nsx + 1) for _ in range(unknowns)]
+    for gy in range(ncy):
+        for gx in range(nsx):
+            number = gy * nsx + gx
+            tile = rate_tiles[gx * nsy + gy // strips]
+            amount = jnp.sum(jnp.where(strip_block == gy % strips, tile, 0.0), axis=0, keepdims=True)
+            amount = jnp.sum(amount, axis=1, keepdims=True)
+            band[number][0] = amount + faces + float(nx * width * nz) * shift_real
+            if gx + 1 < nsx:
+                band[number][1] = jnp.full((1, total), couple_x, jnp.float32)
+            if gy + 1 < ncy:
+                extra = jnp.full((1, total), couple_y, jnp.float32)
+                before = band[number][nsx]
+                band[number][nsx] = extra if before is None else before + extra
+    inverses = []
+    ratios = []
+    for i in range(unknowns):
+        inverse = 1.0 / band[i][0]
+        inverses.append(inverse)
+        ratios.append([None] * (nsx + 1))
+        for a in range(1, nsx + 1):
+            if band[i][a] is None or i + a >= unknowns:
+                continue
+            ratio = band[i][a] * inverse
+            ratios[i][a] = ratio
+            for b in range(a, nsx + 1):
+                if band[i][b] is None or i + b >= unknowns:
+                    continue
+                term = ratio * band[i][b]
+                before = band[i + a][b - a]
+                band[i + a][b - a] = -term if before is None else before - term
+
+
+    exchange_wait(0)
+    for number in range(1, 4):
+        recurrence(number)
+        for offset in range(1, teams):
+            last_copy(number, offset).start()
+        for offset in range(1, teams):
+            last_copy(number, offset).wait()
+        if number < 3:
+            complete(number, history(number))
+            exchange_start(number)
+            exchange_wait(number)
+
+    entry = history(3)
+
+    def finish(moment, state):
+        state = list(state)
+        layer = jnp.zeros((nx, lanes), jnp.float32)
+        for z in range(nz):
+            state[z] = decay[z] * state[z]
+            values = iterate_3[moment, z] + state[z]
+            iterate_3[moment, z] = values
+            layer = layer + (values - iterate_2[moment, z])
+        layer_sums[pl.ds(pl.multiple_of(moment * nx, nx), nx), :] = layer
+        return tuple(state)
+
+    lax.fori_loop(0, moments, finish, tuple(entry[z] for z in range(nz)), unroll=4)
+    by_row = [layer_sums[pl.ds(x, moments, stride=nx), :] for x in range(nx)]
+    columns = sum(by_row[1:], by_row[0])
+    moment_lane = lax.broadcasted_iota(jnp.int32, (moments, lanes), 1)
+    balance = 4.0 * columns - by_row[0] - by_row[nx - 1]
+    balance = balance + jnp.where(moment_lane > 0, pltpu.roll(columns, 1, 1), 0.0)
+    balance = balance + jnp.where(
+        moment_lane < lanes - 1, pltpu.roll(columns, lanes - 1, 1), 0.0
+    )
+    stacked = jnp.concatenate([balance, by_row[0], by_row[nx - 1], columns], axis=0)
+    member = (lane_id // width == row_id).astype(jnp.float32)
+    ends = jnp.where(
+        row_id == 0, first_lane.astype(jnp.float32), last_lane.astype(jnp.float32)
+    )
+    ends = jnp.where(row_id < 2, ends, 0.0)
+
+    def against(left_side, right_side):
+        return lax.dot_general(
+            left_side,
+            right_side,
+            (((1,), (1,)), ((), ())),
+            precision=highest,
+            preferred_element_type=jnp.float32,
+        )
+
+    coarse_tiles[me] = jnp.where(
+        lane_id < 3 * moments, against(member, stacked), against(ends, stacked)
+    )
+
+    def coarse_copy(offset):
+        return pltpu.make_async_remote_copy(
+            src_ref=coarse_tiles.at[me],
+            dst_ref=coarse_tiles.at[me],
+            send_sem=coarse_send.at[offset],
+            recv_sem=coarse_recv.at[offset],
+            device_id=place((me + offset) % devices),
+            device_id_type=pl.DeviceIdType.MESH,
+        )
+
+    def coarse_start(offset, carry):
+        coarse_copy(offset).start()
+        return carry
+
+    def coarse_wait(offset, carry):
+        coarse_copy(offset).wait()
+        return carry
+
+    lax.fori_loop(1, devices, coarse_start, 0)
+    lax.fori_loop(1, devices, coarse_wait, 0)
+
+    kinds = [[None] * spatial for _ in range(4)]
+    quarter = lane_id // moments
+    for slot in range(spatial):
+        for kind in range(4):
+            merged = None
+            for team in range(teams):
+                tile = coarse_tiles[team * spatial + slot]
+                turn = (moments * (team - kind)) % lanes
+                turned = pltpu.roll(tile, turn, 1) if turn else tile
+                merged = turned if team == 0 else jnp.where(quarter == team, turned, merged)
+            kinds[kind][slot] = merged
+    tiles = []
+    for gx in range(nsx):
+        for gy in range(nsy):
+            slot = gx * nsy + gy
+            tile = kinds[0][slot]
+            if gx + 1 < nsx:
+                tile = tile + kinds[1][slot + nsy]
+            if gx > 0:
+                tile = tile + kinds[2][slot - nsy]
+            if gy > 0:
+                tile = tile + jnp.where(row_id == 0, kinds[3][slot - 1][1:2], 0.0)
+            if gy + 1 < nsy:
+                tile = tile + jnp.where(row_id == strips - 1, kinds[3][slot + 1][0:1], 0.0)
+            tiles.append(tile)
+    spectrum = jnp.dot(
+        jnp.concatenate(tiles, axis=0),
+        table_ref[0:total, :],
+        precision=highest,
+        preferred_element_type=jnp.float32,
+    )
+    right = []
+    for gy in range(ncy):
+        for gx in range(nsx):
+            row = (gx * nsy + gy // strips) * nx + gy % strips
+            right.append(spectrum[row : row + 1])
+    for i in range(unknowns):
+        for a in range(1, nsx + 1):
+            if ratios[i][a] is not None:
+                right[i + a] = right[i + a] - ratios[i][a] * right[i]
+    for i in reversed(range(unknowns)):
+        value = right[i] * inverses[i]
+        for a in range(1, nsx + 1):
+            if ratios[i][a] is not None:
+                value = value - ratios[i][a] * right[i + a]
+        right[i] = value
+    for gx in range(nsx):
+        for block in range(nsy):
+            for d in range(strips):
+                number = (block * strips + d) * nsx + gx
+                solved_tiles[gx * nsy + block, d : d + 1, :] = right[number]
+    own_rows = solved_tiles[here]
+    spread = jnp.concatenate(
+        [jnp.broadcast_to(own_rows[d : d + 1], (width, total)) for d in range(strips)], axis=0
+    )
+    own_moments = pl.ds(pl.multiple_of(total + tm * moments, moments), moments)
+    added_ref[...] = against(table_ref[own_moments, :], spread)
+
+    def write(moment, carry):
+        added = added_ref[pl.ds(moment, 1), :]
+        for z in range(nz):
+            out_ref[moment, z] = iterate_3[moment, z] + added
+        return carry
+
+    lax.fori_loop(0, moments, write, 0, unroll=4)
+
+
+def local_fused(teams, nsx, nsy, driving_input, regime, reaction_rates):
+    moments, nz, nx, lanes = driving_input.shape
+    width = AGGREGATE_YCELLS
+    total = teams * moments
+    table = time_tables(total)
+    sizes = (teams, nsx, nsy, moments, nz, nx, lanes, width)
+    devices = teams * nsx * nsy
+    blocks = 2 * moments * nz // lanes
+    f32 = jnp.float32
+    whole = pltpu.VMEM(driving_input.shape, f32)
+    in_hbm = pl.BlockSpec(memory_space=pltpu.HBM)
+    dma = pltpu.SemaphoreType.DMA
+    return pl.pallas_call(
+        functools.partial(fused_kernel, sizes),
+        out_shape=jax.ShapeDtypeStruct(driving_input.shape, f32),
+        in_specs=[pl.BlockSpec(memory_space=pltpu.SMEM)] + [in_hbm] * 3,
+        out_specs=pl.BlockSpec(memory_space=pltpu.VMEM),
+        scratch_shapes=[
+            whole,
+            pltpu.VMEM(regime.shape, jnp.int32),
+            pltpu.VMEM(table.shape, f32),
+            pltpu.VMEM((nsx * nsy, nx, lanes), f32),
+            pltpu.VMEM((devices, 8, total), f32),
+            pltpu.VMEM((nsx * nsy, max(lanes // width, 8), total), f32),
+            pltpu.VMEM((moments, lanes), f32),
+            pltpu.VMEM((moments * nx, lanes), f32),
+            whole,
+            whole,
+            whole,
+            whole,
+            pltpu.VMEM((4, teams, nz, nx, lanes), f32),
+            pltpu.VMEM((3, 2, moments * nz, lanes), f32),
+            pltpu.VMEM((3, 2, moments * nz, lanes), f32),
+            pltpu.VMEM((3, blocks, nx, lanes), f32),
+            pltpu.VMEM((3, 2, blocks, nx, lanes), f32),
+            dma((3,)),
+            dma((4 * teams,)),
+            dma((4 * teams,)),
+            dma((nsx * nsy,)),
+            dma((nsx * nsy,)),
+            dma((devices,)),
+            dma((devices,)),
+            dma((12,)),
+            dma((12,)),
+        ],
+        compiler_params=pltpu.CompilerParams(
+            collective_id=0, has_side_effects=True, vmem_limit_bytes=32 * 1024 * 1024
+        ),
+    )(reaction_rates, driving_input, regime, jnp.asarray(table))
+
+
+def local(driving_input, regime, reaction_rates):
+    moments, nz, nx, lanes = driving_input.shape
+    teams, nsx, nsy = (lax.axis_size(axis) for axis in ("tm", "sx", "sy"))
+    strips = lanes // AGGREGATE_YCELLS
+    whole_strips = nx == AGGREGATE_XCELLS and strips * AGGREGATE_YCELLS == lanes and strips <= 8
+    tiled = nx == 8 and nz == 8 and lanes == 128 and moments % 8 == 0
+    if whole_strips and tiled and teams * moments == 128 and 4 * moments == 128 and SWEEPS == 4:
+        return local_fused(teams, nsx, nsy, driving_input, regime, reaction_rates)
+    return local_general(driving_input, regime, reaction_rates)
+
+
 def solution(mesh):
     placed = (P("tm", None, "sx", "sy"), P(None, "sx", "sy"), P())
     return jax.shard_map(

time: 451 us -> 48.6 us (0.11); the launches traced: 443 us -> 48.3 us
  waiting for transfers between devices: 126 us -> 0 us
  local copies, waits for them, and re-layouts: 123 us -> 4.51 us
  other arithmetic: 95.7 us -> 0 us
  starting transfers between devices: 56.5 us -> 0 us
  Pallas kernels: 0 us -> 43.8 us
  matrix products: 16.5 us -> 0 us
  between operations: 14.5 us -> 0.01 us
  blocking collectives: 10.6 us -> 0 us
    all_gather x2 -> x0, waiting for transfers between devices: 126 us -> none  [the longest x1 85 us: local(): lax.all_gather(unrolled_array, 'tm', axis=1, tiled=True)]
    slice x14 -> x0, local copies, waits for them, and re-layouts: 59.7 us -> none  [the longest x8 34.2 us: extended(): lax.slice_in_dim(block, 0, width, axis=dim)]
    ppermute x16 -> x0, starting transfers between devices: 44.4 us -> none  [the longest x8 33.2 us: extended(): lax.ppermute(lax.slice_in_dim(block, block.shape[dim] - width, None, axis...]
    pallas_call x0 -> x1, Pallas kernels: none -> 43.8 us  [local_fused(): pl.pallas_call(functools.partial(fused_kernel, sizes), out_shape=jax.Shap...]
    ppermute x8 -> x0, local copies, waits for them, and re-layouts: 42 us -> none  [the longest x4 21.1 us: extended(): lax.ppermute(lax.slice_in_dim(block, block.shape[dim] - width, None, axis...]
    another operation x11 -> x0, other arithmetic: 36.4 us -> none  [the longest x4 13.2 us: local(): factor = jnp.linalg.cholesky(system)]
    add x9 -> x0, other arithmetic: 31.2 us -> none  [the longest x3 24.1 us: local(): source_term + neighbors(present_guess)]
    dot_general x4 -> x0, matrix products: 16.1 us -> none  [matmul(): jnp.dot(left_side, right_side, precision=lax.Precision.HIGHEST, preferred...]
  transfers between devices with their start and end apart: 20 -> 0, of which waited for: 2 -> 0; matrix products, arithmetic and copies ran while one was open for 26% -> 0% of each run, Pallas kernels for 0% -> 0%
where the time goes in v3:
time: 48.6 us; the launch traced here: 48.3 us
  Pallas kernels  43.8 us (90%)
  local copies, waits for them, and re-layouts  4.51 us (9%)
    pallas_call x1, Pallas kernels, local_fused(): pl.pallas_call(functools.partial(fused_kernel, sizes), out_shape=jax.Shap...  43.8 us
    unnamed x9, local copies, waits for them, and re-layouts  4.51 us

profile of v3, /device:TPU:0, one launch (start us, length us, event | category | flops | bytes accessed | tf_op | source)
XLA Modules:
  0.0 48.3 jit_solution(14780510974461648481)
XLA Ops:
  0.0 0.0 copy-start
  0.0 1.2 %copy-done = f32[32,8,8,128]{3,2,1,0:T(8,128)S(1)} copy-done((f32[32,8,8,128]{3,2,1,0:T(8,128)S(1)}, f32[32,8,8,128]{3,2,1,0:T(8,128)}, u32[]{:S(2)}) %copy-start) | copy-done | bytes 1048600
  1.2 0.0 copy-start.1
  1.2 0.9 %copy-done.1 = f32[264,128]{1,0:T(8,128)S(1)} copy-done((f32[264,128]{1,0:T(8,128)S(1)}, f32[264,128]{1,0:T(8,128)}, u32[]{:S(2)}) %copy-start.1) | copy-done | bytes 135192
  2.1 0.0 copy-start.2
  2.1 0.8 %copy-done.2 = s32[8,8,128]{2,1,0:T(8,128)S(1)} copy-done((s32[8,8,128]{2,1,0:T(8,128)S(1)}, s32[8,8,128]{2,1,0:T(8,128)}, u32[]{:S(2)}) %copy-start.2) | copy-done | bytes 32792
  2.9 0.0 copy-start.3
  2.9 0.7 %copy-done.3 = f32[8]{0:T(128)S(1)} copy-done((f32[8]{0:T(128)S(1)}, f32[8]{0:T(128)}, u32[]{:S(2)}) %copy-start.3) | copy-done | bytes 56
  3.5 43.8 %shard_map.46 = f32[32,8,8,128]{3,2,1,0:T(8,128)S(1)} custom-call(f32[8]{0:T(128)S(1)} %copy-done.3, f32[32,8,8,128]{3,2,1,0:T(8,128)S(1)} %copy-done, s32[8,8,128]{2,1,0:T(8,128)S(1)} %copy-done.2, f32[264,128]{1,0:T(8,128)S(1)} %copy-done.1), custom_call_target="tpu_custom_call" | custom-call | tf_op jit(solution)/shard_map/pallas_call | solution.py:671
  47.4 1.0 %copy.6 = f32[32,8,8,128]{3,2,1,0:T(8,128)} copy(f32[32,8,8,128]{3,2,1,0:T(8,128)S(1)} %shard_map.46) | data formatting | bytes 2097152
Async XLA Ops:
  0.0 1.2 %copy-start = (f32[32,8,8,128]{3,2,1,0:T(8,128)S(1)}, f32[32,8,8,128]{3,2,1,0:T(8,128)}, u32[]{:S(2)}) copy-start(f32[32,8,8,128]{3,2,1,0:T(8,128)} %field_hbm.1) | copy-start | bytes 3145732
  1.2 0.9 %copy-start.1 = (f32[264,128]{1,0:T(8,128)S(1)}, f32[264,128]{1,0:T(8,128)}, u32[]{:S(2)}) copy-start(f32[264,128]{1,0:T(8,128)} %constant.2.clone.table_hbm) | copy-start | bytes 405508
  2.1 0.8 %copy-start.2 = (s32[8,8,128]{2,1,0:T(8,128)S(1)}, s32[8,8,128]{2,1,0:T(8,128)}, u32[]{:S(2)}) copy-start(s32[8,8,128]{2,1,0:T(8,128)} %regime_hbm.1) | copy-start | bytes 98308
  2.9 0.7 %copy-start.3 = (f32[8]{0:T(128)S(1)}, f32[8]{0:T(128)}, u32[]{:S(2)}) copy-start(f32[8]{0:T(128)} %rates_ref.1) | copy-start | bytes 100

commit v4 on v3

--- a/solution.py
+++ b/solution.py
@@ -239,6 +239,13 @@
     x_halos,
     y_edges,
     y_halos,
+    y_ends,
+    x_lasts,
+    y_lasts,
+    x_edge_decay,
+    x_halo_decay,
+    y_edge_decay,
+    y_halo_decay,
     load_sem,
     last_send,
     last_recv,
@@ -248,6 +255,10 @@
     coarse_recv,
     halo_send,
     halo_recv,
+    diagonal_send,
+    diagonal_recv,
+    decay_send,
+    decay_recv,
 ):
     teams, nsx, nsy, moments, nz, nx, lanes, width = sizes
     total = teams * moments
@@ -297,17 +308,22 @@
         rates = rates + jnp.where(regime == number, rates_ref[number], 0.0)
     rate_tiles[here] = jnp.sum(rates, axis=0)
     decay = 1.0 / (rates + 7.0)
-    decay_block = jnp.ones_like(decay)
-    power, left = decay, moments
-    while left:
-        if left & 1:
-            decay_block = decay_block * power
-        power = power * power
-        left //= 2
-    decay_round = jnp.ones_like(decay)
-    for _ in range(teams):
-        decay_round = decay_round * decay_block
-    closing = 1.0 / (1.0 - decay_round)
+
+    def raised(value, exponent):
+        result = jnp.ones_like(value)
+        while exponent:
+            if exponent & 1:
+                result = result * value
+            value = value * value
+            exponent //= 2
+        return result
+
+    def history(decay_of, part):
+        decay_block = raised(decay_of, moments)
+        value = part(0)
+        for offset in range(1, teams):
+            value = part(offset) + decay_block * value
+        return value / (1.0 - raised(decay_block, teams))
 
     has = (ix > 0, ix < nsx - 1, iy > 0, iy < nsy - 1)
     neighbour = (
@@ -322,6 +338,14 @@
             @pl.when(jnp.logical_not(has[side]))
             def _(halo=(x_halos if side < 2 else y_halos).at[number, side % 2]):
                 halo[...] = jnp.zeros(halo.shape, jnp.float32)
+
+    for side in (2, 3):
+
+        @pl.when(jnp.logical_not(has[side]))
+        def _(side=side):
+            y_halo_decay[side % 2] = jnp.zeros((nx, lanes), jnp.float32)
+            for number in range(3):
+                y_lasts[number, side % 2] = jnp.zeros((teams, nx, lanes), jnp.float32)
 
     def halo_copies(number):
         copies = []
@@ -344,15 +368,56 @@
             )
         return copies
 
-    def exchange_start(number):
-        for side, copy in enumerate(halo_copies(number)):
+    def decay_copies():
+        copies = []
+        for side in range(4):
+            if side < 2:
+                source = x_edge_decay.at[side]
+                target = x_halo_decay.at[1 - side]
+            else:
+                source = y_edge_decay
+                target = y_halo_decay.at[3 - side]
+            copies.append(
+                pltpu.make_async_remote_copy(
+                    src_ref=source,
+                    dst_ref=target,
+                    send_sem=decay_send.at[side],
+                    recv_sem=decay_recv.at[side ^ 1],
+                    device_id=neighbour[side],
+                    device_id_type=pl.DeviceIdType.MESH,
+                )
+            )
+        return copies
+
+    def diagonal_copies(number, offset):
+        copies = []
+        for side in range(4):
+            if side < 2:
+                source = x_edges.at[number, side, pl.ds((moments - 1) * nz, nz)]
+                target = x_lasts.at[number, 1 - side, tm]
+            else:
+                source = y_edges.at[number, moments // chunk - 1]
+                target = y_lasts.at[number, 3 - side, tm]
+            copies.append(
+                pltpu.make_async_remote_copy(
+                    src_ref=source,
+                    dst_ref=target,
+                    send_sem=diagonal_send.at[(number * 4 + side) * teams + offset],
+                    recv_sem=diagonal_recv.at[(number * 4 + (side ^ 1)) * teams + offset],
+                    device_id={**neighbour[side], "tm": (tm + offset) % teams},
+                    device_id_type=pl.DeviceIdType.MESH,
+                )
+            )
+        return copies
+
+    def start_all(copies):
+        for side, copy in enumerate(copies):
 
             @pl.when(has[side])
             def _(copy=copy):
                 copy.start()
 
-    def exchange_wait(number):
-        copies = halo_copies(number)
+    def wait_all(copies):
         for side in range(4):
 
             @pl.when(has[side])
@@ -393,22 +458,21 @@
     def recurrence(number):
         def body(block, state):
             if number:
-                high = y_halos[number - 1, 1, block]
-                low = pltpu.roll(y_halos[number - 1, 0, block], 2, 1)
-                ends = jnp.where(odd_lane, low, high)
+                ends = y_ends[block]
                 old = iterates[number - 1]
             state = list(state)
+            packed = jnp.zeros((nx, lanes), jnp.float32)
             for inner in range(chunk):
                 moment = block * chunk + inner
                 if number:
                     cells = [old[moment, z] for z in range(nz)]
                 for z in range(nz):
                     values = field_ref[moment, z]
+                    slot = inner * nz + z
+                    row = moment * nz + z
                     if number:
                         here_cell = cells[z]
-                        slot = inner * nz + z
                         turned = pltpu.roll(ends, (lanes - 2 * slot - 1) % lanes, 1)
-                        row = moment * nz + z
                         low_row = x_halos[number - 1, 0, pl.ds(row, 1), :]
                         high_row = x_halos[number - 1, 1, pl.ds(row, 1), :]
                         values = values + cells[z - 1] + cells[(z + 1) % nz]
@@ -426,6 +490,14 @@
                         )
                     state[z] = decay[z] * (values + state[z])
                     iterates[number][moment, z] = state[z]
+                    if number < 3:
+                        packed = jnp.where(
+                            pair == slot, pltpu.roll(state[z], 2 * slot, 1), packed
+                        )
+                        x_edges[number, 0, pl.ds(row, 1), :] = state[z][0:1]
+                        x_edges[number, 1, pl.ds(row, 1), :] = state[z][nx - 1 : nx]
+            if number < 3:
+                y_edges[number, block] = packed
             return tuple(state)
 
         start = tuple(jnp.zeros((nx, lanes), jnp.float32) for _ in range(nz))
@@ -433,44 +505,105 @@
         for z in range(nz):
             lasts[number, tm, z] = state[z]
 
-    def history(number):
-        value = lasts[number, tm]
+    def own_history(number):
+        return history(decay, lambda offset: lasts[number, (tm + offset) % teams])
+
+    def complete(number):
+        entry = own_history(number)
+
+        def body(moment, state):
+            state = list(state)
+            for z in range(nz):
+                state[z] = decay[z] * state[z]
+                iterates[number][moment, z] = iterates[number][moment, z] + state[z]
+            return tuple(state)
+
+        lax.fori_loop(0, moments, body, tuple(entry[z] for z in range(nz)), unroll=4)
+
+    def merge(low, high):
+        return jnp.where(odd_lane, pltpu.roll(low, 2, 1), high)
+
+    def repeat(values):
+        values = jnp.where(lane_id // (2 * nz) == chunk - 1, values, 0.0)
+        turn = 2 * nz
+        while turn < lanes:
+            values = values + pltpu.roll(values, turn, 1)
+            turn *= 2
+        return values
+
+    def correct_halos(number):
+        for side in range(2):
+
+            @pl.when(has[side])
+            def _(side=side):
+                decay_of = x_halo_decay[side]
+
+                def part(offset):
+                    if offset == 0:
+                        return x_halos[number, side, pl.ds((moments - 1) * nz, nz), :]
+                    return x_lasts[number, side, (tm + offset) % teams]
+
+                def body(moment, state):
+                    state = decay_of * state
+                    at = pl.ds(pl.multiple_of(moment * nz, nz), nz)
+                    x_halos[number, side, at, :] = x_halos[number, side, at, :] + state
+                    return state
+
+                lax.fori_loop(0, moments, body, history(decay_of, part), unroll=8)
+
+        final = moments // chunk - 1
+        decay_of = repeat(merge(y_halo_decay[0], y_halo_decay[1]))
+
+        def part(offset):
+            if offset == 0:
+                return merge(y_halos[number, 0, final], y_halos[number, 1, final])
+            team = (tm + offset) % teams
+            return merge(y_lasts[number, 0, team], y_lasts[number, 1, team])
+
+        entry = repeat(history(decay_of, part))
+        power = decay_of
+        for inner in range(1, chunk):
+            power = jnp.where(lane_id // (2 * nz) >= inner, power * decay_of, power)
+        state = power * entry
+        for block in range(moments // chunk):
+            y_ends[block] = merge(y_halos[number, 0, block], y_halos[number, 1, block]) + state
+            state = state * raised(decay_of, chunk)
+
+    def send(number):
+        start_all(halo_copies(number))
         for offset in range(1, teams):
-            value = lasts[number, (tm + offset) % teams] + decay_block * value
-        return value * closing
-
-    def complete(number, entry):
-        def body(block, state):
-            state = list(state)
-            packed = jnp.zeros((nx, lanes), jnp.float32)
-            for inner in range(chunk):
-                moment = block * chunk + inner
-                for z in range(nz):
-                    state[z] = decay[z] * state[z]
-                    values = iterates[number][moment, z] + state[z]
-                    iterates[number][moment, z] = values
-                    slot = inner * nz + z
-                    packed = jnp.where(pair == slot, pltpu.roll(values, 2 * slot, 1), packed)
-                    row = moment * nz + z
-                    x_edges[number, 0, pl.ds(row, 1), :] = values[0:1]
-                    x_edges[number, 1, pl.ds(row, 1), :] = values[nx - 1 : nx]
-            y_edges[number, block] = packed
-            return tuple(state)
-
-        lax.fori_loop(0, moments // chunk, body, tuple(entry[z] for z in range(nz)))
-
+            last_copy(number, offset).start()
+        for offset in range(1, teams):
+            start_all(diagonal_copies(number, offset))
+
+    def receive_lasts(number):
+        for offset in range(1, teams):
+            last_copy(number, offset).wait()
+
+    def receive_halos(number):
+        wait_all(halo_copies(number))
+        for offset in range(1, teams):
+            wait_all(diagonal_copies(number, offset))
+        correct_halos(number)
+
+    packed_decay = jnp.zeros((nx, lanes), jnp.float32)
+    for z in range(nz):
+        x_edge_decay[0, z : z + 1, :] = decay[z, 0:1]
+        x_edge_decay[1, z : z + 1, :] = decay[z, nx - 1 : nx]
+        slot = (chunk - 1) * nz + z
+        packed_decay = jnp.where(
+            pair == slot, pltpu.roll(decay[z], 2 * slot, 1), packed_decay
+        )
+    y_edge_decay[...] = packed_decay
     loads[1].wait()
     recurrence(0)
     pl.semaphore_wait(barrier, devices - 1)
-    for offset in range(1, teams):
-        last_copy(0, offset).start()
+    send(0)
+    start_all(decay_copies())
     for offset in range(1, spatial):
         rate_copy(offset).start()
-    for offset in range(1, teams):
-        last_copy(0, offset).wait()
-    complete(0, history(0))
-    exchange_start(0)
-
+    receive_lasts(0)
+    complete(0)
     for offset in range(1, spatial):
         rate_copy(offset).wait()
     loads[2].wait()
@@ -514,19 +647,19 @@
                 band[i + a][b - a] = -term if before is None else before - term
 
 
-    exchange_wait(0)
-    for number in range(1, 4):
+    wait_all(decay_copies())
+    receive_halos(0)
+    for number in range(1, 3):
         recurrence(number)
-        for offset in range(1, teams):
-            last_copy(number, offset).start()
-        for offset in range(1, teams):
-            last_copy(number, offset).wait()
-        if number < 3:
-            complete(number, history(number))
-            exchange_start(number)
-            exchange_wait(number)
-
-    entry = history(3)
+        send(number)
+        receive_lasts(number)
+        complete(number)
+        receive_halos(number)
+    recurrence(3)
+    for offset in range(1, teams):
+        last_copy(3, offset).start()
+    receive_lasts(3)
+    entry = own_history(3)
 
     def finish(moment, state):
         state = list(state)
@@ -691,6 +824,13 @@
             pltpu.VMEM((3, 2, moments * nz, lanes), f32),
             pltpu.VMEM((3, blocks, nx, lanes), f32),
             pltpu.VMEM((3, 2, blocks, nx, lanes), f32),
+            pltpu.VMEM((blocks, nx, lanes), f32),
+            pltpu.VMEM((3, 2, teams, nz, lanes), f32),
+            pltpu.VMEM((3, 2, teams, nx, lanes), f32),
+            pltpu.VMEM((2, nz, lanes), f32),
+            pltpu.VMEM((2, nz, lanes), f32),
+            pltpu.VMEM((nx, lanes), f32),
+            pltpu.VMEM((2, nx, lanes), f32),
             dma((3,)),
             dma((4 * teams,)),
             dma((4 * teams,)),
@@ -700,9 +840,13 @@
             dma((devices,)),
             dma((12,)),
             dma((12,)),
+            dma((12 * teams,)),
+            dma((12 * teams,)),
+            dma((4,)),
+            dma((4,)),
         ],
         compiler_params=pltpu.CompilerParams(
-            collective_id=0, has_side_effects=True, vmem_limit_bytes=32 * 1024 * 1024
+            collective_id=0, has_side_effects=True, vmem_limit_bytes=62 * 1024 * 1024
         ),
     )(reaction_rates, driving_input, regime, jnp.asarray(table))
 

time: 48.6 us -> 56.6 us (1.16)
  Pallas kernels: 43.8 us -> 54.1 us
  local copies, waits for them, and re-layouts: 4.51 us -> 2.31 us
    pallas_call x1, Pallas kernels: 43.8 us -> 54.1 us  [local_fused(): pl.pallas_call(functools.partial(fused_kernel, sizes), out_shape=jax.Shap...]
    unnamed x9 -> x1, local copies, waits for them, and re-layouts: 4.51 us -> 2.31 us
where the time goes in v4:
time: 56.6 us; the launch traced here: 56.4 us
  Pallas kernels  54.1 us (96%)
  local copies, waits for them, and re-layouts  2.31 us (4%)
    pallas_call x1, Pallas kernels, local_fused(): pl.pallas_call(functools.partial(fused_kernel, sizes), out_shape=jax.Shap...  54.1 us
    unnamed x1, local copies, waits for them, and re-layouts  2.31 us

profile of v4, /device:TPU:0, one launch (start us, length us, event | category | flops | bytes accessed | tf_op | source)
XLA Modules:
  0.0 56.4 jit_solution(6464157401505761113)
XLA Ops:
  0.0 54.1 %shard_map.46 = f32[32,8,8,128]{3,2,1,0:T(8,128)} custom-call(f32[8]{0:T(128)} %rates_ref.1, f32[32,8,8,128]{3,2,1,0:T(8,128)} %field_hbm.1, s32[8,8,128]{2,1,0:T(8,128)} %regime_hbm.1, f32[264,128]{1,0:T(8,128)} %constant.2.clone.table_hbm), custom_call_target="tpu_custom_call" | custom-call | tf_op jit(solution)/shard_map/pallas_call | solution.py:804
  54.1 2.3 %copy.6 = f32[32,8,8,128]{3,2,1,0:T(8,128)} copy(f32[32,8,8,128]{3,2,1,0:T(8,128)} %shard_map.46) | data formatting | bytes 2097152

commit v5 on v3

--- a/solution.py
+++ b/solution.py
@@ -221,14 +221,15 @@
     field_hbm,
     regime_hbm,
     table_hbm,
-    out_ref,
+    out_hbm,
+    added_ref,
     field_ref,
     regime_ref,
     table_ref,
     rate_tiles,
     coarse_tiles,
+    all_kinds,
     solved_tiles,
-    added_ref,
     layer_sums,
     iterate_0,
     iterate_1,
@@ -240,12 +241,15 @@
     y_edges,
     y_halos,
     load_sem,
+    store_sem,
     last_send,
     last_recv,
     rate_send,
     rate_recv,
-    coarse_send,
-    coarse_recv,
+    team_send,
+    team_recv,
+    kind_send,
+    kind_recv,
     halo_send,
     halo_recv,
 ):
@@ -254,13 +258,11 @@
     strips = lanes // width
     plane = nz * nx
     spatial = nsx * nsy
-    devices = teams * spatial
     highest = lax.Precision.HIGHEST
     tm = lax.axis_index("tm")
     ix = lax.axis_index("sx")
     iy = lax.axis_index("sy")
     here = ix * nsy + iy
-    me = tm * spatial + here
 
     loads = [
         pltpu.make_async_copy(regime_hbm, regime_ref, load_sem.at[0]),
@@ -270,32 +272,56 @@
     for load in loads:
         load.start()
 
-    def place(rank):
-        return {
-            "tm": rank // spatial,
-            "sx": (rank % spatial) // nsy,
-            "sy": rank % nsy,
-        }
-
+    def peers(axis, index, size):
+        return [{"tm": tm, "sx": ix, "sy": iy, axis: (index + o) % size} for o in range(1, size)]
+
+    team_peers = peers("tm", tm, teams)
+    row_peers = peers("sx", ix, nsx)
+    strip_peers = peers("sy", iy, nsy)
+    greeted = team_peers + row_peers + strip_peers
     barrier = pltpu.get_barrier_semaphore()
-
-    def greet(offset, carry):
+    for peer in greeted:
         pl.semaphore_signal(
-            barrier,
-            inc=1,
-            device_id=place((me + offset) % devices),
-            device_id_type=pl.DeviceIdType.MESH,
+            barrier, inc=1, device_id=peer, device_id_type=pl.DeviceIdType.MESH
         )
-        return carry
-
-    lax.fori_loop(1, devices, greet, 0)
+
+    def gather(ref, targets, send_sem, recv_sem, first):
+        return [
+            pltpu.make_async_remote_copy(
+                src_ref=ref,
+                dst_ref=ref,
+                send_sem=send_sem.at[first + number],
+                recv_sem=recv_sem.at[first + number],
+                device_id=peer,
+                device_id_type=pl.DeviceIdType.MESH,
+            )
+            for number, peer in enumerate(targets)
+        ]
+
+    def spatial_gather(ref, send_sem, recv_sem):
+        def whole():
+            for copy in gather(ref.at[iy, ix], row_peers, send_sem, recv_sem, 0):
+                copy.start()
+            for copy in gather(ref.at[iy, ix], row_peers, send_sem, recv_sem, 0):
+                copy.wait()
+            for copy in gather(ref.at[iy], strip_peers, send_sem, recv_sem, nsx):
+                copy.start()
+
+        def finish():
+            for copy in gather(ref.at[iy], strip_peers, send_sem, recv_sem, nsx):
+                copy.wait()
+
+        return whole, finish
 
     loads[0].wait()
     rates = jnp.zeros(regime_ref.shape, jnp.float32)
     regime = regime_ref[...]
     for number in range(rates_ref.shape[0]):
         rates = rates + jnp.where(regime == number, rates_ref[number], 0.0)
-    rate_tiles[here] = jnp.sum(rates, axis=0)
+    rate_tiles[iy, ix] = jnp.sum(rates, axis=0)
+    pl.semaphore_wait(barrier, len(greeted))
+    rates_begin, rates_end = spatial_gather(rate_tiles, rate_send, rate_recv)
+    rates_begin()
     decay = 1.0 / (rates + 7.0)
     decay_block = jnp.ones_like(decay)
     power, left = decay, moments
@@ -359,17 +385,6 @@
             def _(side=side):
                 copies[side].wait_send()
                 copies[side ^ 1].wait_recv()
-
-    def rate_copy(offset):
-        peer = (here + offset) % spatial
-        return pltpu.make_async_remote_copy(
-            src_ref=rate_tiles.at[here],
-            dst_ref=rate_tiles.at[here],
-            send_sem=rate_send.at[offset],
-            recv_sem=rate_recv.at[offset],
-            device_id={"tm": tm, "sx": peer // nsy, "sy": peer % nsy},
-            device_id_type=pl.DeviceIdType.MESH,
-        )
 
     def last_copy(number, offset):
         return pltpu.make_async_remote_copy(
@@ -461,18 +476,14 @@
 
     loads[1].wait()
     recurrence(0)
-    pl.semaphore_wait(barrier, devices - 1)
     for offset in range(1, teams):
         last_copy(0, offset).start()
-    for offset in range(1, spatial):
-        rate_copy(offset).start()
     for offset in range(1, teams):
         last_copy(0, offset).wait()
     complete(0, history(0))
     exchange_start(0)
 
-    for offset in range(1, spatial):
-        rate_copy(offset).wait()
+    rates_end()
     loads[2].wait()
     shift_real = table_ref[2 * total : 2 * total + 1, :]
     ncy = nsy * strips
@@ -485,7 +496,7 @@
     for gy in range(ncy):
         for gx in range(nsx):
             number = gy * nsx + gx
-            tile = rate_tiles[gx * nsy + gy // strips]
+            tile = rate_tiles[gy // strips, gx]
             amount = jnp.sum(jnp.where(strip_block == gy % strips, tile, 0.0), axis=0, keepdims=True)
             amount = jnp.sum(amount, axis=1, keepdims=True)
             band[number][0] = amount + faces + float(nx * width * nz) * shift_real
@@ -540,6 +551,8 @@
         return tuple(state)
 
     lax.fori_loop(0, moments, finish, tuple(entry[z] for z in range(nz)), unroll=4)
+    store = pltpu.make_async_copy(iterate_3, out_hbm, store_sem)
+    store.start()
     by_row = [layer_sums[pl.ds(x, moments, stride=nx), :] for x in range(nx)]
     columns = sum(by_row[1:], by_row[0])
     moment_lane = lax.broadcasted_iota(jnp.int32, (moments, lanes), 1)
@@ -564,42 +577,29 @@
             preferred_element_type=jnp.float32,
         )
 
-    coarse_tiles[me] = jnp.where(
+    coarse_tiles[tm] = jnp.where(
         lane_id < 3 * moments, against(member, stacked), against(ends, stacked)
     )
-
-    def coarse_copy(offset):
-        return pltpu.make_async_remote_copy(
-            src_ref=coarse_tiles.at[me],
-            dst_ref=coarse_tiles.at[me],
-            send_sem=coarse_send.at[offset],
-            recv_sem=coarse_recv.at[offset],
-            device_id=place((me + offset) % devices),
-            device_id_type=pl.DeviceIdType.MESH,
-        )
-
-    def coarse_start(offset, carry):
-        coarse_copy(offset).start()
-        return carry
-
-    def coarse_wait(offset, carry):
-        coarse_copy(offset).wait()
-        return carry
-
-    lax.fori_loop(1, devices, coarse_start, 0)
-    lax.fori_loop(1, devices, coarse_wait, 0)
-
-    kinds = [[None] * spatial for _ in range(4)]
+    for copy in gather(coarse_tiles.at[tm], team_peers, team_send, team_recv, 0):
+        copy.start()
+    for copy in gather(coarse_tiles.at[tm], team_peers, team_send, team_recv, 0):
+        copy.wait()
     quarter = lane_id // moments
-    for slot in range(spatial):
-        for kind in range(4):
-            merged = None
-            for team in range(teams):
-                tile = coarse_tiles[team * spatial + slot]
-                turn = (moments * (team - kind)) % lanes
-                turned = pltpu.roll(tile, turn, 1) if turn else tile
-                merged = turned if team == 0 else jnp.where(quarter == team, turned, merged)
-            kinds[kind][slot] = merged
+    for kind in range(4):
+        merged = None
+        for team in range(teams):
+            tile = coarse_tiles[team]
+            turn = (moments * (team - kind)) % lanes
+            turned = pltpu.roll(tile, turn, 1) if turn else tile
+            merged = turned if team == 0 else jnp.where(quarter == team, turned, merged)
+        all_kinds[iy, ix, kind] = merged
+    kinds_begin, kinds_end = spatial_gather(all_kinds, kind_send, kind_recv)
+    kinds_begin()
+    kinds_end()
+    kinds = [
+        [all_kinds[slot % nsy, slot // nsy, kind] for slot in range(spatial)]
+        for kind in range(4)
+    ]
     tiles = []
     for gx in range(nsx):
         for gy in range(nsy):
@@ -647,13 +647,7 @@
     own_moments = pl.ds(pl.multiple_of(total + tm * moments, moments), moments)
     added_ref[...] = against(table_ref[own_moments, :], spread)
 
-    def write(moment, carry):
-        added = added_ref[pl.ds(moment, 1), :]
-        for z in range(nz):
-            out_ref[moment, z] = iterate_3[moment, z] + added
-        return carry
-
-    lax.fori_loop(0, moments, write, 0, unroll=4)
+    store.wait()
 
 
 def local_fused(teams, nsx, nsy, driving_input, regime, reaction_rates):
@@ -662,25 +656,27 @@
     total = teams * moments
     table = time_tables(total)
     sizes = (teams, nsx, nsy, moments, nz, nx, lanes, width)
-    devices = teams * nsx * nsy
     blocks = 2 * moments * nz // lanes
     f32 = jnp.float32
     whole = pltpu.VMEM(driving_input.shape, f32)
     in_hbm = pl.BlockSpec(memory_space=pltpu.HBM)
     dma = pltpu.SemaphoreType.DMA
-    return pl.pallas_call(
+    field, added = pl.pallas_call(
         functools.partial(fused_kernel, sizes),
-        out_shape=jax.ShapeDtypeStruct(driving_input.shape, f32),
+        out_shape=(
+            jax.ShapeDtypeStruct(driving_input.shape, f32),
+            jax.ShapeDtypeStruct((moments, lanes), f32),
+        ),
         in_specs=[pl.BlockSpec(memory_space=pltpu.SMEM)] + [in_hbm] * 3,
-        out_specs=pl.BlockSpec(memory_space=pltpu.VMEM),
+        out_specs=(pl.BlockSpec(memory_space=pl.ANY), pl.BlockSpec(memory_space=pltpu.VMEM)),
         scratch_shapes=[
             whole,
             pltpu.VMEM(regime.shape, jnp.int32),
             pltpu.VMEM(table.shape, f32),
-            pltpu.VMEM((nsx * nsy, nx, lanes), f32),
-            pltpu.VMEM((devices, 8, total), f32),
+            pltpu.VMEM((nsy, nsx, nx, lanes), f32),
+            pltpu.VMEM((teams, 8, total), f32),
+            pltpu.VMEM((nsy, nsx, 4, 8, total), f32),
             pltpu.VMEM((nsx * nsy, max(lanes // width, 8), total), f32),
-            pltpu.VMEM((moments, lanes), f32),
             pltpu.VMEM((moments * nx, lanes), f32),
             whole,
             whole,
@@ -692,19 +688,23 @@
             pltpu.VMEM((3, blocks, nx, lanes), f32),
             pltpu.VMEM((3, 2, blocks, nx, lanes), f32),
             dma((3,)),
+            dma,
             dma((4 * teams,)),
             dma((4 * teams,)),
-            dma((nsx * nsy,)),
-            dma((nsx * nsy,)),
-            dma((devices,)),
-            dma((devices,)),
+            dma((nsx + nsy,)),
+            dma((nsx + nsy,)),
+            dma((teams,)),
+            dma((teams,)),
+            dma((nsx + nsy,)),
+            dma((nsx + nsy,)),
             dma((12,)),
             dma((12,)),
         ],
         compiler_params=pltpu.CompilerParams(
-            collective_id=0, has_side_effects=True, vmem_limit_bytes=32 * 1024 * 1024
+            collective_id=0, has_side_effects=True, vmem_limit_bytes=62 * 1024 * 1024
         ),
     )(reaction_rates, driving_input, regime, jnp.asarray(table))
+    return field + added[:, None, None, :]
 
 
 def local(driving_input, regime, reaction_rates):

time: 48.6 us -> 49.7 us (1.023)
  local copies, waits for them, and re-layouts: 4.51 us -> 0 us
  Pallas kernels: 43.8 us -> 47.3 us
  other arithmetic: 0 us -> 2.29 us
    unnamed x9 -> x0, local copies, waits for them, and re-layouts: 4.51 us -> none
    pallas_call x1, Pallas kernels: 43.8 us -> 47.3 us  [local_fused(): pl.pallas_call(functools.partial(fused_kernel, sizes), out_shape=(jax.Sha...]
    add x0 -> x1, other arithmetic: none -> 2.29 us  [local_fused(): return field + added[:, None, None, :]]
where the time goes in v5:
time: 49.7 us; the launch traced here: 49.6 us
  Pallas kernels  47.3 us (95%)
  other arithmetic  2.29 us (5%)
    pallas_call x1, Pallas kernels, local_fused(): pl.pallas_call(functools.partial(fused_kernel, sizes), out_shape=(jax.Sha...  47.3 us
    add x1, other arithmetic, local_fused(): return field + added[:, None, None, :]  2.29 us

profile of v5, /device:TPU:0, one launch (start us, length us, event | category | flops | bytes accessed | tf_op | source)
XLA Modules:
  0.0 49.6 jit_solution(9546088620518981610)
XLA Ops:
  0.0 47.3 %shard_map.46 = (f32[32,8,8,128]{3,2,1,0:T(8,128)}, f32[32,128]{1,0:T(8,128)}) custom-call(f32[8]{0:T(128)} %rates_ref.1, f32[32,8,8,128]{3,2,1,0:T(8,128)} %field_hbm.1, s32[8,8,128]{2,1,0:T(8,128)} %regime_hbm.1, f32[264,128]{1,0:T(8,128)} %constant.2.clone.table_hbm), custom_call_target="tpu_custom_call" | custom-call | tf_op jit(solution)/shard_map/pallas_call | solution.py:664
  47.3 2.3 %broadcast_add_fusion = f32[32,8,8,128]{3,2,1,0:T(8,128)} fusion(f32[32,8,8,128]{3,2,1,0:T(8,128)} %get-tuple-element.7, f32[32,128]{1,0:T(8,128)} %get-tuple-element.8), kind=kLoop, calls=%fused_computation | loop fusion | flops 262144 | bytes 2113536 | tf_op jit(solution)/shard_map/add | solution.py:707

commit v6 on v3

--- a/solution.py
+++ b/solution.py
@@ -221,14 +221,14 @@
     field_hbm,
     regime_hbm,
     table_hbm,
-    out_ref,
+    out_hbm,
+    added_ref,
     field_ref,
     regime_ref,
     table_ref,
     rate_tiles,
     coarse_tiles,
     solved_tiles,
-    added_ref,
     layer_sums,
     iterate_0,
     iterate_1,
@@ -240,6 +240,7 @@
     y_edges,
     y_halos,
     load_sem,
+    store_sem,
     last_send,
     last_recv,
     rate_send,
@@ -381,6 +382,9 @@
             device_id_type=pl.DeviceIdType.MESH,
         )
 
+    def cell(moment, z):
+        return pl.ds(pl.multiple_of((moment * nz + z) * nx, nx), nx)
+
     iterates = (iterate_0, iterate_1, iterate_2, iterate_3)
     chunk = lanes // 2 // nz
     row_id = lax.broadcasted_iota(jnp.int32, (nx, lanes), 0)
@@ -401,16 +405,15 @@
             for inner in range(chunk):
                 moment = block * chunk + inner
                 if number:
-                    cells = [old[moment, z] for z in range(nz)]
+                    cells = [old[cell(moment, z), :] for z in range(nz)]
                 for z in range(nz):
                     values = field_ref[moment, z]
                     if number:
                         here_cell = cells[z]
                         slot = inner * nz + z
                         turned = pltpu.roll(ends, (lanes - 2 * slot - 1) % lanes, 1)
-                        row = moment * nz + z
-                        low_row = x_halos[number - 1, 0, pl.ds(row, 1), :]
-                        high_row = x_halos[number - 1, 1, pl.ds(row, 1), :]
+                        low_row = x_halos[number - 1, 0, moment, z : z + 1, :]
+                        high_row = x_halos[number - 1, 1, moment, z : z + 1, :]
                         values = values + cells[z - 1] + cells[(z + 1) % nz]
                         values = values + jnp.where(
                             first_row, low_row, pltpu.roll(here_cell, 1, 0)
@@ -425,7 +428,7 @@
                             last_lane, turned, pltpu.roll(here_cell, lanes - 1, 1)
                         )
                     state[z] = decay[z] * (values + state[z])
-                    iterates[number][moment, z] = state[z]
+                    iterates[number][cell(moment, z), :] = state[z]
             return tuple(state)
 
         start = tuple(jnp.zeros((nx, lanes), jnp.float32) for _ in range(nz))
@@ -447,13 +450,13 @@
                 moment = block * chunk + inner
                 for z in range(nz):
                     state[z] = decay[z] * state[z]
-                    values = iterates[number][moment, z] + state[z]
-                    iterates[number][moment, z] = values
+                    values = iterates[number][cell(moment, z), :] + state[z]
+                    iterates[number][cell(moment, z), :] = values
                     slot = inner * nz + z
                     packed = jnp.where(pair == slot, pltpu.roll(values, 2 * slot, 1), packed)
-                    row = moment * nz + z
-                    x_edges[number, 0, pl.ds(row, 1), :] = values[0:1]
-                    x_edges[number, 1, pl.ds(row, 1), :] = values[nx - 1 : nx]
+                for side, edge_row in enumerate((0, nx - 1)):
+                    rows = pl.ds(moment * plane + edge_row, nz, stride=nx)
+                    x_edges[number, side, moment] = iterates[number][rows, :]
             y_edges[number, block] = packed
             return tuple(state)
 
@@ -533,13 +536,15 @@
         layer = jnp.zeros((nx, lanes), jnp.float32)
         for z in range(nz):
             state[z] = decay[z] * state[z]
-            values = iterate_3[moment, z] + state[z]
-            iterate_3[moment, z] = values
-            layer = layer + (values - iterate_2[moment, z])
+            values = iterate_3[cell(moment, z), :] + state[z]
+            iterate_3[cell(moment, z), :] = values
+            layer = layer + (values - iterate_2[cell(moment, z), :])
         layer_sums[pl.ds(pl.multiple_of(moment * nx, nx), nx), :] = layer
         return tuple(state)
 
     lax.fori_loop(0, moments, finish, tuple(entry[z] for z in range(nz)), unroll=4)
+    store = pltpu.make_async_copy(iterate_3, out_hbm, store_sem)
+    store.start()
     by_row = [layer_sums[pl.ds(x, moments, stride=nx), :] for x in range(nx)]
     columns = sum(by_row[1:], by_row[0])
     moment_lane = lax.broadcasted_iota(jnp.int32, (moments, lanes), 1)
@@ -647,13 +652,7 @@
     own_moments = pl.ds(pl.multiple_of(total + tm * moments, moments), moments)
     added_ref[...] = against(table_ref[own_moments, :], spread)
 
-    def write(moment, carry):
-        added = added_ref[pl.ds(moment, 1), :]
-        for z in range(nz):
-            out_ref[moment, z] = iterate_3[moment, z] + added
-        return carry
-
-    lax.fori_loop(0, moments, write, 0, unroll=4)
+    store.wait()
 
 
 def local_fused(teams, nsx, nsy, driving_input, regime, reaction_rates):
@@ -666,13 +665,17 @@
     blocks = 2 * moments * nz // lanes
     f32 = jnp.float32
     whole = pltpu.VMEM(driving_input.shape, f32)
+    flat = pltpu.VMEM((moments * nz * nx, lanes), f32)
     in_hbm = pl.BlockSpec(memory_space=pltpu.HBM)
     dma = pltpu.SemaphoreType.DMA
-    return pl.pallas_call(
+    field, added = pl.pallas_call(
         functools.partial(fused_kernel, sizes),
-        out_shape=jax.ShapeDtypeStruct(driving_input.shape, f32),
+        out_shape=(
+            pltpu.VMEM((moments * nz * nx, lanes), f32),
+            pltpu.VMEM((moments, lanes), f32),
+        ),
         in_specs=[pl.BlockSpec(memory_space=pltpu.SMEM)] + [in_hbm] * 3,
-        out_specs=pl.BlockSpec(memory_space=pltpu.VMEM),
+        out_specs=(pl.BlockSpec(memory_space=pl.ANY), pl.BlockSpec(memory_space=pltpu.VMEM)),
         scratch_shapes=[
             whole,
             pltpu.VMEM(regime.shape, jnp.int32),
@@ -680,18 +683,18 @@
             pltpu.VMEM((nsx * nsy, nx, lanes), f32),
             pltpu.VMEM((devices, 8, total), f32),
             pltpu.VMEM((nsx * nsy, max(lanes // width, 8), total), f32),
-            pltpu.VMEM((moments, lanes), f32),
             pltpu.VMEM((moments * nx, lanes), f32),
-            whole,
-            whole,
-            whole,
-            whole,
+            flat,
+            flat,
+            flat,
+            flat,
             pltpu.VMEM((4, teams, nz, nx, lanes), f32),
-            pltpu.VMEM((3, 2, moments * nz, lanes), f32),
-            pltpu.VMEM((3, 2, moments * nz, lanes), f32),
+            pltpu.VMEM((3, 2, moments, nz, lanes), f32),
+            pltpu.VMEM((3, 2, moments, nz, lanes), f32),
             pltpu.VMEM((3, blocks, nx, lanes), f32),
             pltpu.VMEM((3, 2, blocks, nx, lanes), f32),
             dma((3,)),
+            dma,
             dma((4 * teams,)),
             dma((4 * teams,)),
             dma((nsx * nsy,)),
@@ -702,9 +705,10 @@
             dma((12,)),
         ],
         compiler_params=pltpu.CompilerParams(
-            collective_id=0, has_side_effects=True, vmem_limit_bytes=32 * 1024 * 1024
+            collective_id=0, has_side_effects=True, vmem_limit_bytes=62 * 1024 * 1024
         ),
     )(reaction_rates, driving_input, regime, jnp.asarray(table))
+    return field.reshape(driving_input.shape) + added[:, None, None, :]
 
 
 def local(driving_input, regime, reaction_rates):

time: 48.6 us -> 44.6 us (0.918)
  local copies, waits for them, and re-layouts: 4.51 us -> 0 us
  other arithmetic: 0 us -> 1.12 us
    unnamed x9 -> x0, local copies, waits for them, and re-layouts: 4.51 us -> none
    add x0 -> x1, other arithmetic: none -> 1.12 us  [local_fused(): return field.reshape(driving_input.shape) + added[:, None, None, :]]
where the time goes in v6:
time: 44.6 us; the launch traced here: 44.5 us
  Pallas kernels  43.4 us (97%)
  other arithmetic  1.12 us (3%)
    pallas_call x1, Pallas kernels, local_fused(): pl.pallas_call(functools.partial(fused_kernel, sizes), out_shape=(pltpu.V...  43.4 us
    add x1, other arithmetic, local_fused(): return field.reshape(driving_input.shape) + added[:, None, None, :]  1.12 us

profile of v6, /device:TPU:0, one launch (start us, length us, event | category | flops | bytes accessed | tf_op | source)
XLA Modules:
  0.0 44.5 jit_solution(3422074166347966456)
XLA Ops:
  0.0 43.4 %shard_map.46 = (f32[2048,128]{1,0:T(8,128)S(1)}, f32[32,128]{1,0:T(8,128)S(1)}) custom-call(f32[8]{0:T(128)} %rates_ref.1, f32[32,8,8,128]{3,2,1,0:T(8,128)} %field_hbm.1, s32[8,8,128]{2,1,0:T(8,128)} %regime_hbm.1, f32[264,128]{1,0:T(8,128)} %constant.2.clone.table_hbm), custom_call_target="tpu_custom_call" | custom-call | tf_op jit(solution)/shard_map/pallas_call | solution.py:671
  43.4 1.1 %broadcast_add_fusion = f32[32,8,8,128]{3,2,1,0:T(8,128)} fusion(f32[32,8,8,128]{3,2,1,0:T(8,128)S(1)} %bitcast.1, f32[32,128]{1,0:T(8,128)S(1)} %get-tuple-element.8), kind=kLoop, calls=%fused_computation | loop fusion | flops 262144 | bytes 2113536 | tf_op jit(solution)/shard_map/add | solution.py:711

commit v7 on v6

--- a/solution.py
+++ b/solution.py
@@ -372,12 +372,19 @@
             device_id_type=pl.DeviceIdType.MESH,
         )
 
-    def last_copy(number, offset):
+    part_planes = nz // 2
+    parts = (0, 1)
+
+    def planes(part):
+        return range(part * part_planes, (part + 1) * part_planes)
+
+    def last_copy(number, part, offset):
+        block = lasts.at[number, tm, pl.ds(part * part_planes, part_planes)]
         return pltpu.make_async_remote_copy(
-            src_ref=lasts.at[number, tm],
-            dst_ref=lasts.at[number, tm],
-            send_sem=last_send.at[number * teams + offset],
-            recv_sem=last_recv.at[number * teams + offset],
+            src_ref=block,
+            dst_ref=block,
+            send_sem=last_send.at[(number * 2 + part) * teams + offset],
+            recv_sem=last_recv.at[(number * 2 + part) * teams + offset],
             device_id={"tm": (tm + offset) % teams, "sx": ix, "sy": iy},
             device_id_type=pl.DeviceIdType.MESH,
         )
@@ -394,7 +401,7 @@
     odd_lane = lane_id % 2 == 1
     pair = (lane_id + 1) % lanes // 2
 
-    def recurrence(number):
+    def recurrence(number, part):
         def body(block, state):
             if number:
                 high = y_halos[number - 1, 1, block]
@@ -405,8 +412,11 @@
             for inner in range(chunk):
                 moment = block * chunk + inner
                 if number:
-                    cells = [old[cell(moment, z), :] for z in range(nz)]
-                for z in range(nz):
+                    cells = {
+                        z % nz: old[cell(moment, z % nz), :]
+                        for z in range(part * part_planes - 1, (part + 1) * part_planes + 1)
+                    }
+                for number_in, z in enumerate(planes(part)):
                     values = field_ref[moment, z]
                     if number:
                         here_cell = cells[z]
@@ -414,7 +424,7 @@
                         turned = pltpu.roll(ends, (lanes - 2 * slot - 1) % lanes, 1)
                         low_row = x_halos[number - 1, 0, moment, z : z + 1, :]
                         high_row = x_halos[number - 1, 1, moment, z : z + 1, :]
-                        values = values + cells[z - 1] + cells[(z + 1) % nz]
+                        values = values + cells[(z - 1) % nz] + cells[(z + 1) % nz]
                         values = values + jnp.where(
                             first_row, low_row, pltpu.roll(here_cell, 1, 0)
                         )
@@ -427,53 +437,57 @@
                         values = values + jnp.where(
                             last_lane, turned, pltpu.roll(here_cell, lanes - 1, 1)
                         )
-                    state[z] = decay[z] * (values + state[z])
-                    iterates[number][cell(moment, z), :] = state[z]
+                    state[number_in] = decay[z] * (values + state[number_in])
+                    iterates[number][cell(moment, z), :] = state[number_in]
             return tuple(state)
 
-        start = tuple(jnp.zeros((nx, lanes), jnp.float32) for _ in range(nz))
+        start = tuple(jnp.zeros((nx, lanes), jnp.float32) for _ in planes(part))
         state = lax.fori_loop(0, moments // chunk, body, start)
-        for z in range(nz):
-            lasts[number, tm, z] = state[z]
-
-    def history(number):
-        value = lasts[number, tm]
+        for number_in, z in enumerate(planes(part)):
+            lasts[number, tm, z] = state[number_in]
         for offset in range(1, teams):
-            value = lasts[number, (tm + offset) % teams] + decay_block * value
-        return value * closing
-
-    def complete(number, entry):
+            last_copy(number, part, offset).start()
+
+    def history(number, part):
+        at = slice(part * part_planes, (part + 1) * part_planes)
+        value = lasts[number, tm, at]
+        for offset in range(1, teams):
+            value = lasts[number, (tm + offset) % teams, at] + decay_block[at] * value
+        return value * closing[at]
+
+    def complete(number, part):
+        for offset in range(1, teams):
+            last_copy(number, part, offset).wait()
+        entry = history(number, part)
+
         def body(block, state):
             state = list(state)
-            packed = jnp.zeros((nx, lanes), jnp.float32)
+            packed = y_edges[number, block] if part else jnp.zeros((nx, lanes), jnp.float32)
             for inner in range(chunk):
                 moment = block * chunk + inner
-                for z in range(nz):
-                    state[z] = decay[z] * state[z]
-                    values = iterates[number][cell(moment, z), :] + state[z]
+                for number_in, z in enumerate(planes(part)):
+                    state[number_in] = decay[z] * state[number_in]
+                    values = iterates[number][cell(moment, z), :] + state[number_in]
                     iterates[number][cell(moment, z), :] = values
                     slot = inner * nz + z
                     packed = jnp.where(pair == slot, pltpu.roll(values, 2 * slot, 1), packed)
-                for side, edge_row in enumerate((0, nx - 1)):
+                for side, edge_row in enumerate((0, nx - 1) if part else ()):
                     rows = pl.ds(moment * plane + edge_row, nz, stride=nx)
                     x_edges[number, side, moment] = iterates[number][rows, :]
             y_edges[number, block] = packed
             return tuple(state)
 
-        lax.fori_loop(0, moments // chunk, body, tuple(entry[z] for z in range(nz)))
+        lax.fori_loop(0, moments // chunk, body, tuple(entry[z] for z in range(part_planes)))
 
     loads[1].wait()
-    recurrence(0)
     pl.semaphore_wait(barrier, devices - 1)
-    for offset in range(1, teams):
-        last_copy(0, offset).start()
+    for part in parts:
+        recurrence(0, part)
     for offset in range(1, spatial):
         rate_copy(offset).start()
-    for offset in range(1, teams):
-        last_copy(0, offset).wait()
-    complete(0, history(0))
+    for part in parts:
+        complete(0, part)
     exchange_start(0)
-
     for offset in range(1, spatial):
         rate_copy(offset).wait()
     loads[2].wait()
@@ -500,36 +514,40 @@
                 band[number][nsx] = extra if before is None else before + extra
     inverses = []
     ratios = []
-    for i in range(unknowns):
-        inverse = 1.0 / band[i][0]
-        inverses.append(inverse)
-        ratios.append([None] * (nsx + 1))
-        for a in range(1, nsx + 1):
-            if band[i][a] is None or i + a >= unknowns:
-                continue
-            ratio = band[i][a] * inverse
-            ratios[i][a] = ratio
-            for b in range(a, nsx + 1):
-                if band[i][b] is None or i + b >= unknowns:
+
+    def factor(count):
+        for i in range(len(inverses), min(unknowns, len(inverses) + count)):
+            inverse = 1.0 / band[i][0]
+            inverses.append(inverse)
+            ratios.append([None] * (nsx + 1))
+            for a in range(1, nsx + 1):
+                if band[i][a] is None or i + a >= unknowns:
                     continue
-                term = ratio * band[i][b]
-                before = band[i + a][b - a]
-                band[i + a][b - a] = -term if before is None else before - term
+                ratio = band[i][a] * inverse
+                ratios[i][a] = ratio
+                for b in range(a, nsx + 1):
+                    if band[i][b] is None or i + b >= unknowns:
+                        continue
+                    term = ratio * band[i][b]
+                    before = band[i + a][b - a]
+                    band[i + a][b - a] = -term if before is None else before - term
 
 
     exchange_wait(0)
+    share = -(-unknowns // 2)
     for number in range(1, 4):
-        recurrence(number)
+        for part in parts:
+            recurrence(number, part)
+        if number < 3:
+            for part in parts:
+                complete(number, part)
+            exchange_start(number)
+            factor(share)
+            exchange_wait(number)
+    for part in parts:
         for offset in range(1, teams):
-            last_copy(number, offset).start()
-        for offset in range(1, teams):
-            last_copy(number, offset).wait()
-        if number < 3:
-            complete(number, history(number))
-            exchange_start(number)
-            exchange_wait(number)
-
-    entry = history(3)
+            last_copy(3, part, offset).wait()
+    entry = jnp.concatenate([history(3, part) for part in parts], axis=0)
 
     def finish(moment, state):
         state = list(state)
@@ -695,8 +713,8 @@
             pltpu.VMEM((3, 2, blocks, nx, lanes), f32),
             dma((3,)),
             dma,
-            dma((4 * teams,)),
-            dma((4 * teams,)),
+            dma((8 * teams,)),
+            dma((8 * teams,)),
             dma((nsx * nsy,)),
             dma((nsx * nsy,)),
             dma((devices,)),

time: 44.6 us -> 45 us (level)
  no operation moved by 1% of the time
where the time goes in v7:
time: 45 us; the launch traced here: 44.8 us
  Pallas kernels  43.7 us (97%)
  other arithmetic  1.12 us (2%)
    pallas_call x1, Pallas kernels, local_fused(): pl.pallas_call(functools.partial(fused_kernel, sizes), out_shape=(pltpu.V...  43.7 us
    add x1, other arithmetic, local_fused(): return field.reshape(driving_input.shape) + added[:, None, None, :]  1.12 us

profile of v7, /device:TPU:0, one launch (start us, length us, event | category | flops | bytes accessed | tf_op | source)
XLA Modules:
  0.0 44.8 jit_solution(12233869732438902373)
XLA Ops:
  0.0 43.7 %shard_map.46 = (f32[2048,128]{1,0:T(8,128)S(1)}, f32[32,128]{1,0:T(8,128)S(1)}) custom-call(f32[8]{0:T(128)} %rates_ref.1, f32[32,8,8,128]{3,2,1,0:T(8,128)} %field_hbm.1, s32[8,8,128]{2,1,0:T(8,128)} %regime_hbm.1, f32[264,128]{1,0:T(8,128)} %constant.2.clone.table_hbm), custom_call_target="tpu_custom_call" | custom-call | tf_op jit(solution)/shard_map/pallas_call | solution.py:689
  43.7 1.1 %broadcast_add_fusion = f32[32,8,8,128]{3,2,1,0:T(8,128)} fusion(f32[32,8,8,128]{3,2,1,0:T(8,128)S(1)} %bitcast.1, f32[32,128]{1,0:T(8,128)S(1)} %get-tuple-element.8), kind=kLoop, calls=%fused_computation | loop fusion | flops 262144 | bytes 2113536 | tf_op jit(solution)/shard_map/add | solution.py:729

commit v8 on v6

--- a/solution.py
+++ b/solution.py
@@ -228,6 +228,7 @@
     table_ref,
     rate_tiles,
     coarse_tiles,
+    all_kinds,
     solved_tiles,
     layer_sums,
     iterate_0,
@@ -247,6 +248,8 @@
     rate_recv,
     coarse_send,
     coarse_recv,
+    kind_send,
+    kind_recv,
     halo_send,
     halo_recv,
 ):
@@ -255,13 +258,11 @@
     strips = lanes // width
     plane = nz * nx
     spatial = nsx * nsy
-    devices = teams * spatial
     highest = lax.Precision.HIGHEST
     tm = lax.axis_index("tm")
     ix = lax.axis_index("sx")
     iy = lax.axis_index("sy")
     here = ix * nsy + iy
-    me = tm * spatial + here
 
     loads = [
         pltpu.make_async_copy(regime_hbm, regime_ref, load_sem.at[0]),
@@ -271,25 +272,31 @@
     for load in loads:
         load.start()
 
-    def place(rank):
-        return {
-            "tm": rank // spatial,
-            "sx": (rank % spatial) // nsy,
-            "sy": rank % nsy,
-        }
-
+    team_peers = [
+        {"tm": (tm + offset) % teams, "sx": ix, "sy": iy} for offset in range(1, teams)
+    ]
+    space_peers = []
+    for offset in range(1, spatial):
+        peer = (here + offset) % spatial
+        space_peers.append({"tm": tm, "sx": peer // nsy, "sy": peer % nsy})
     barrier = pltpu.get_barrier_semaphore()
-
-    def greet(offset, carry):
+    for peer in team_peers + space_peers:
         pl.semaphore_signal(
-            barrier,
-            inc=1,
-            device_id=place((me + offset) % devices),
-            device_id_type=pl.DeviceIdType.MESH,
-        )
-        return carry
-
-    lax.fori_loop(1, devices, greet, 0)
+            barrier, inc=1, device_id=peer, device_id_type=pl.DeviceIdType.MESH
+        )
+
+    def gather(ref, targets, send_sem, recv_sem):
+        return [
+            pltpu.make_async_remote_copy(
+                src_ref=ref,
+                dst_ref=ref,
+                send_sem=send_sem.at[number],
+                recv_sem=recv_sem.at[number],
+                device_id=peer,
+                device_id_type=pl.DeviceIdType.MESH,
+            )
+            for number, peer in enumerate(targets)
+        ]
 
     loads[0].wait()
     rates = jnp.zeros(regime_ref.shape, jnp.float32)
@@ -464,7 +471,7 @@
 
     loads[1].wait()
     recurrence(0)
-    pl.semaphore_wait(barrier, devices - 1)
+    pl.semaphore_wait(barrier, len(team_peers) + len(space_peers))
     for offset in range(1, teams):
         last_copy(0, offset).start()
     for offset in range(1, spatial):
@@ -500,24 +507,27 @@
                 band[number][nsx] = extra if before is None else before + extra
     inverses = []
     ratios = []
-    for i in range(unknowns):
-        inverse = 1.0 / band[i][0]
-        inverses.append(inverse)
-        ratios.append([None] * (nsx + 1))
-        for a in range(1, nsx + 1):
-            if band[i][a] is None or i + a >= unknowns:
-                continue
-            ratio = band[i][a] * inverse
-            ratios[i][a] = ratio
-            for b in range(a, nsx + 1):
-                if band[i][b] is None or i + b >= unknowns:
+
+    def factor(count):
+        for i in range(len(inverses), min(unknowns, len(inverses) + count)):
+            inverse = 1.0 / band[i][0]
+            inverses.append(inverse)
+            ratios.append([None] * (nsx + 1))
+            for a in range(1, nsx + 1):
+                if band[i][a] is None or i + a >= unknowns:
                     continue
-                term = ratio * band[i][b]
-                before = band[i + a][b - a]
-                band[i + a][b - a] = -term if before is None else before - term
+                ratio = band[i][a] * inverse
+                ratios[i][a] = ratio
+                for b in range(a, nsx + 1):
+                    if band[i][b] is None or i + b >= unknowns:
+                        continue
+                    term = ratio * band[i][b]
+                    before = band[i + a][b - a]
+                    band[i + a][b - a] = -term if before is None else before - term
 
 
     exchange_wait(0)
+    share = -(-unknowns // 2)
     for number in range(1, 4):
         recurrence(number)
         for offset in range(1, teams):
@@ -527,6 +537,7 @@
         if number < 3:
             complete(number, history(number))
             exchange_start(number)
+            factor(share)
             exchange_wait(number)
 
     entry = history(3)
@@ -569,42 +580,29 @@
             preferred_element_type=jnp.float32,
         )
 
-    coarse_tiles[me] = jnp.where(
+    coarse_tiles[tm] = jnp.where(
         lane_id < 3 * moments, against(member, stacked), against(ends, stacked)
     )
-
-    def coarse_copy(offset):
-        return pltpu.make_async_remote_copy(
-            src_ref=coarse_tiles.at[me],
-            dst_ref=coarse_tiles.at[me],
-            send_sem=coarse_send.at[offset],
-            recv_sem=coarse_recv.at[offset],
-            device_id=place((me + offset) % devices),
-            device_id_type=pl.DeviceIdType.MESH,
-        )
-
-    def coarse_start(offset, carry):
-        coarse_copy(offset).start()
-        return carry
-
-    def coarse_wait(offset, carry):
-        coarse_copy(offset).wait()
-        return carry
-
-    lax.fori_loop(1, devices, coarse_start, 0)
-    lax.fori_loop(1, devices, coarse_wait, 0)
-
-    kinds = [[None] * spatial for _ in range(4)]
+    copies = gather(coarse_tiles.at[tm], team_peers, coarse_send, coarse_recv)
+    for copy in copies:
+        copy.start()
+    for copy in copies:
+        copy.wait()
     quarter = lane_id // moments
-    for slot in range(spatial):
-        for kind in range(4):
-            merged = None
-            for team in range(teams):
-                tile = coarse_tiles[team * spatial + slot]
-                turn = (moments * (team - kind)) % lanes
-                turned = pltpu.roll(tile, turn, 1) if turn else tile
-                merged = turned if team == 0 else jnp.where(quarter == team, turned, merged)
-            kinds[kind][slot] = merged
+    for kind in range(4):
+        merged = None
+        for team in range(teams):
+            tile = coarse_tiles[team]
+            turn = (moments * (team - kind)) % lanes
+            turned = pltpu.roll(tile, turn, 1) if turn else tile
+            merged = turned if team == 0 else jnp.where(quarter == team, turned, merged)
+        all_kinds[here, kind] = merged
+    copies = gather(all_kinds.at[here], space_peers, kind_send, kind_recv)
+    for copy in copies:
+        copy.start()
+    for copy in copies:
+        copy.wait()
+    kinds = [[all_kinds[slot, kind] for slot in range(spatial)] for kind in range(4)]
     tiles = []
     for gx in range(nsx):
         for gy in range(nsy):
@@ -661,7 +659,6 @@
     total = teams * moments
     table = time_tables(total)
     sizes = (teams, nsx, nsy, moments, nz, nx, lanes, width)
-    devices = teams * nsx * nsy
     blocks = 2 * moments * nz // lanes
     f32 = jnp.float32
     whole = pltpu.VMEM(driving_input.shape, f32)
@@ -681,7 +678,8 @@
             pltpu.VMEM(regime.shape, jnp.int32),
             pltpu.VMEM(table.shape, f32),
             pltpu.VMEM((nsx * nsy, nx, lanes), f32),
-            pltpu.VMEM((devices, 8, total), f32),
+            pltpu.VMEM((teams, 8, total), f32),
+            pltpu.VMEM((nsx * nsy, 4, 8, total), f32),
             pltpu.VMEM((nsx * nsy, max(lanes // width, 8), total), f32),
             pltpu.VMEM((moments * nx, lanes), f32),
             flat,
@@ -699,8 +697,10 @@
             dma((4 * teams,)),
             dma((nsx * nsy,)),
             dma((nsx * nsy,)),
-            dma((devices,)),
-            dma((devices,)),
+            dma((teams,)),
+            dma((teams,)),
+            dma((nsx * nsy,)),
+            dma((nsx * nsy,)),
             dma((12,)),
             dma((12,)),
         ],

time: 44.6 us -> 45.7 us (1.025)
  Pallas kernels: 43.4 us -> 44.5 us
    pallas_call x1, Pallas kernels: 43.4 us -> 44.5 us  [local_fused(): pl.pallas_call(functools.partial(fused_kernel, sizes), out_shape=(pltpu.V...]
where the time goes in v8:
time: 45.7 us; the launch traced here: 45.6 us
  Pallas kernels  44.5 us (97%)
  other arithmetic  1.12 us (2%)
    pallas_call x1, Pallas kernels, local_fused(): pl.pallas_call(functools.partial(fused_kernel, sizes), out_shape=(pltpu.V...  44.5 us
    add x1, other arithmetic, local_fused(): return field.reshape(driving_input.shape) + added[:, None, None, :]  1.12 us

profile of v8, /device:TPU:0, one launch (start us, length us, event | category | flops | bytes accessed | tf_op | source)
XLA Modules:
  0.0 45.6 jit_solution(11248026359849850033)
XLA Ops:
  0.0 44.5 %shard_map.46 = (f32[2048,128]{1,0:T(8,128)S(1)}, f32[32,128]{1,0:T(8,128)S(1)}) custom-call(f32[8]{0:T(128)} %rates_ref.1, f32[32,8,8,128]{3,2,1,0:T(8,128)} %field_hbm.1, s32[8,8,128]{2,1,0:T(8,128)} %regime_hbm.1, f32[264,128]{1,0:T(8,128)} %constant.2.clone.table_hbm), custom_call_target="tpu_custom_call" | custom-call | tf_op jit(solution)/shard_map/pallas_call | solution.py:668
  44.5 1.1 %broadcast_add_fusion = f32[32,8,8,128]{3,2,1,0:T(8,128)} fusion(f32[32,8,8,128]{3,2,1,0:T(8,128)S(1)} %bitcast.1, f32[32,128]{1,0:T(8,128)S(1)} %get-tuple-element.8), kind=kLoop, calls=%fused_computation | loop fusion | flops 262144 | bytes 2113536 | tf_op jit(solution)/shard_map/add | solution.py:711

commit v9 on v6

--- a/solution.py
+++ b/solution.py
@@ -542,7 +542,7 @@
         layer_sums[pl.ds(pl.multiple_of(moment * nx, nx), nx), :] = layer
         return tuple(state)
 
-    lax.fori_loop(0, moments, finish, tuple(entry[z] for z in range(nz)), unroll=4)
+    lax.fori_loop(0, moments, finish, tuple(entry[z] for z in range(nz)), unroll=8)
     store = pltpu.make_async_copy(iterate_3, out_hbm, store_sem)
     store.start()
     by_row = [layer_sums[pl.ds(x, moments, stride=nx), :] for x in range(nx)]

time: 44.6 us -> 44.6 us (level)
  no operation moved by 1% of the time
where the time goes in v9:
time: 44.6 us; the launch traced here: 44.5 us
  Pallas kernels  43.3 us (97%)
  other arithmetic  1.12 us (3%)
    pallas_call x1, Pallas kernels, local_fused(): pl.pallas_call(functools.partial(fused_kernel, sizes), out_shape=(pltpu.V...  43.3 us
    add x1, other arithmetic, local_fused(): return field.reshape(driving_input.shape) + added[:, None, None, :]  1.12 us

profile of v9, /device:TPU:0, one launch (start us, length us, event | category | flops | bytes accessed | tf_op | source)
XLA Modules:
  0.0 44.5 jit_solution(3808244428266719344)
XLA Ops:
  0.0 43.3 %shard_map.46 = (f32[2048,128]{1,0:T(8,128)S(1)}, f32[32,128]{1,0:T(8,128)S(1)}) custom-call(f32[8]{0:T(128)} %rates_ref.1, f32[32,8,8,128]{3,2,1,0:T(8,128)} %field_hbm.1, s32[8,8,128]{2,1,0:T(8,128)} %regime_hbm.1, f32[264,128]{1,0:T(8,128)} %constant.2.clone.table_hbm), custom_call_target="tpu_custom_call" | custom-call | tf_op jit(solution)/shard_map/pallas_call | solution.py:671
  43.4 1.1 %broadcast_add_fusion = f32[32,8,8,128]{3,2,1,0:T(8,128)} fusion(f32[32,8,8,128]{3,2,1,0:T(8,128)S(1)} %bitcast.1, f32[32,128]{1,0:T(8,128)S(1)} %get-tuple-element.8), kind=kLoop, calls=%fused_computation | loop fusion | flops 262144 | bytes 2113536 | tf_op jit(solution)/shard_map/add | solution.py:711
